TPU v7x, 256 devices: a whole 4x4x8 slice. The times are simulated.
256 devices in a mesh: row: 16 (over z, y_lo), col: 16 (over x, y_hi, core).
Axes of the slice: x: 4, y: 4 (y_hi: 2, y_lo: 2; y = y_hi * 2 + y_lo), z: 8, core: 2. Of those that a mesh axis runs over, the one named last changes fastest.
Arguments:
- z_band: bfloat16 [1024, 768, 128], P('row', 'col'), may hold values from -6 to 6
- z_square: bfloat16 [768, 768, 128], P('row', 'col'), may hold values from -6 to 6
- ln_in_gain: float32 [128], replicated, may hold values from 0.1 to 1.9
- w_a_gate: bfloat16 [128, 128], replicated, may hold values from -0.5 to 0.5
- w_a: bfloat16 [128, 128], replicated, may hold values from -0.5 to 0.5
- w_b_gate: bfloat16 [128, 128], replicated, may hold values from -0.5 to 0.5
- w_b: bfloat16 [128, 128], replicated, may hold values from -0.5 to 0.5
- w_g: bfloat16 [128, 128], replicated, may hold values from -0.5 to 0.5
- ln_out_gain: float32 [128], replicated, may hold values from 0.1 to 1.9
- w_out: bfloat16 [128, 128], replicated, may hold values from -0.5 to 0.5
Outputs:
- update: bfloat16 [1024, 768, 128], P('row', 'col')
All inputs are finite; a program needn't handle non-finite values.
Results may differ from a plain program's by a relative error of at most 0.022.
Values may be sent and summed in bfloat16 or wider, within the bound.
No kernel may reach another device: no remote copies, remote signals or barrier semaphores. Data moves between devices by JAX's collectives and lax.ppermute only.
A program may use at most 128 MiB of HBM per device.

v0:
```python
import functools

import jax
import jax.numpy as jnp
from jax import lax
from jax.experimental import pallas as pl
from jax.experimental.pallas import tpu as pltpu
from jax.sharding import Mesh, PartitionSpec as P

F32 = jnp.float32
BF16 = jnp.bfloat16
PARTS = (("z", 8), ("y_lo", 2), ("x", 4), ("y_hi", 2), ("core", 2))
CHIPS = ("z", "y_lo", "x", "y_hi")
ROWS = 16
COLS = 8
LANES = 128
MESSAGE = 42
VMEM = 40 * 1024 * 1024


def params():
    return pltpu.CompilerParams(vmem_limit_bytes=VMEM)


def layer_norm(values, gain):
    mean = jnp.mean(values, axis=-1, keepdims=True)
    centred = values - mean
    var = jnp.mean(centred * centred, axis=-1, keepdims=True)
    return centred * lax.rsqrt(var + 1e-05) * gain


def swap(arrays):
    lane = lax.broadcasted_iota(jnp.int32, arrays[0].shape, len(arrays[0].shape) - 1)
    axis = len(arrays[0].shape) - 1
    arrays = list(arrays)
    for bit in range(3):
        shift = 16 << bit
        low = (lane & shift) == 0
        for first in range(8):
            if first & (1 << bit):
                continue
            second = first | (1 << bit)
            a, b = arrays[first], arrays[second]
            arrays[first] = jnp.where(low, a, pltpu.roll(b, shift, axis))
            arrays[second] = jnp.where(low, pltpu.roll(a, LANES - shift, axis), b)
    return arrays


def edges_kernel(
    band_hbm, square_hbm, gain_hbm, wag_hbm, wa_hbm, wbg_hbm, wb_hbm, out_ref,
    band, square, gain_ref, weights, normed, held, sems,
):
    quarter = band.shape[0] // 4
    parts = [slice(n * quarter, n * quarter + quarter) for n in range(4)]
    pairs = [(gain_hbm, gain_ref)]
    pairs += [(band_hbm.at[part], band.at[part]) for part in parts]
    pairs += [
        (wag_hbm, weights.at[0]),
        (wa_hbm, weights.at[1]),
        (wbg_hbm, weights.at[2]),
        (wb_hbm, weights.at[3]),
        (square_hbm, square),
    ]
    copies = [pltpu.make_async_copy(a, b, sems.at[n]) for n, (a, b) in enumerate(pairs)]
    for copy in copies:
        copy.start()
    share = jnp.full((LANES, LANES), 1.0 / LANES, BF16)
    copies[0].wait()
    gain = gain_ref[...]

    def project(both, rows):
        both = lax.dot_general(both, rows, (((1,), (1,)), ((), ())), preferred_element_type=F32)
        return jax.nn.sigmoid(both[:LANES]) * both[LANES:]

    for part in range(24):
        if part % 6 == 0:
            copies[1 + part // 6].wait()
        rows = slice(part * LANES, part * LANES + LANES)
        z = band[rows, :]
        centred = z.astype(F32) - jnp.dot(z, share, preferred_element_type=F32)
        squares = (centred * centred).astype(BF16)
        var = jnp.dot(squares, share, preferred_element_type=F32)
        normed[rows, :] = centred * lax.rsqrt(var + 1e-05) * gain
    for copy in copies[5:]:
        copy.wait()
    left = jnp.concatenate([weights[0].T, weights[1].T], axis=0)
    right = jnp.concatenate([weights[2].T, weights[3].T], axis=0)
    for step in range(12):
        rows = [
            normed[pl.ds(bit * 24 + step * 2 + odd, 64, stride=48), :]
            for odd in range(2)
            for bit in range(2)
        ]
        edge = project(left, jnp.concatenate(rows, axis=0).astype(BF16))
        for odd in range(2):
            kb, kk = divmod(step * 2 + odd, 8)
            held[pl.ds(kk * 3 + kb, LANES, stride=MESSAGE), :] = edge[
                :, odd * LANES : odd * LANES + LANES
            ]
        if step < 9:
            k3, hi = step // 3, step % 3 * 2
            z = square[hi * 8 : hi * 8 + 16, k3 * 16 : k3 * 16 + 16, :].reshape(2 * LANES, LANES)
            edge = project(right, layer_norm(z.astype(F32), gain).astype(BF16))
            for odd in range(2):
                held[pl.ds(24 + (hi + odd) * 3 + k3, LANES, stride=MESSAGE), :] = edge[
                    :, odd * LANES : odd * LANES + LANES
                ]
    out_ref[...] = held[...].astype(BF16)


def swap_halves(a, b):
    low = lax.broadcasted_iota(jnp.int32, a.shape, 1) < 64
    moved = pltpu.roll(jnp.where(low, b, a), 64, 1)
    return jnp.where(low, a, moved), jnp.where(low, moved, b)


def product_kernel(core_ref, in_ref, own_ref, other_ref, left, right, raw, held):
    size = 32 * MESSAGE

    def quad(p, carry):
        raw[:size, :] = in_ref[pl.ds(pl.multiple_of(p * size, 16), size), :].astype(F32)

        def rows(n, start):
            return raw[pl.ds(n * MESSAGE + start, 8, stride=3), :]

        for half in range(2):
            for q in range(8):
                n = half * 16 + q
                pairs = [swap_halves(rows(n, kb), rows(n + 8, kb)) for kb in range(3)]
                blocks = [pair[kbit] for kbit in range(2) for pair in pairs]
                for k3 in range(3):
                    left[
                        p,
                        k3 * LANES + q * 16 : k3 * LANES + q * 16 + 16,
                        half * LANES : half * LANES + LANES,
                    ] = jnp.concatenate(blocks[2 * k3 : 2 * k3 + 2], axis=0).astype(BF16)
        for n in range(4):
            for k3 in range(3):
                blocks = swap([rows(n * 8 + q, 24 + k3) for q in range(8)])
                for lo in range(8):
                    held[n, lo * 24 + k3 * 8 : lo * 24 + k3 * 8 + 8, :] = blocks[lo]
        for core in range(2):
            for k3 in range(3):
                for hi in range(6):
                    tiles = [
                        held[half * 2 + core, pl.ds(k3 * 8 + hi, 8, stride=24), :]
                        for half in range(2)
                    ]
                    right[
                        core,
                        pl.ds(pl.multiple_of(hi * 64 + p * 16, 16), 16),
                        k3 * LANES : k3 * LANES + LANES,
                    ] = jnp.concatenate(tiles, axis=0).astype(BF16)
        return carry

    lax.fori_loop(0, 4, quad, 0)
    core = core_ref[0]
    for which, ref in ((1 - core, other_ref), (core, own_ref)):
        for p in range(4):
            ref[:, p * 256 : p * 256 + 256] = jnp.dot(
                right[which], left[p], preferred_element_type=F32
            ).astype(ref.dtype)


def sum_kernel(own_ref, other_ref, out_ref):
    for p in range(8):
        lanes = slice(p * LANES, p * LANES + LANES)
        for q2 in range(4):
            tiles = []
            for jh in range(3):
                a, b = [
                    own_ref[start : start + 16, lanes] + other_ref[start : start + 16, lanes].astype(F32)
                    for start in (jh * 64 + q2 * 16, 192 + jh * 64 + q2 * 16)
                ]
                tiles.append(swap_halves(a, b))
            for odd in range(2):
                for n in range(2):
                    out_ref[(p * 2 + odd) * 8 + q2 * 2 + n] = jnp.concatenate(
                        [tiles[jh][odd][n * 8 : n * 8 + 8] for jh in range(3)], axis=0
                    ).astype(BF16)


def gate_kernel(band_ref, gain_ref, wg_ref, out_ref):
    normed = layer_norm(band_ref[...].astype(F32), gain_ref[...]).astype(BF16)
    out_ref[...] = jax.nn.sigmoid(jnp.dot(normed, wg_ref[...], preferred_element_type=F32))


def update_kernel(in_ref, gate_ref, gain_ref, wout_ref, out_ref, held, result):
    held[...] = in_ref[...].astype(F32).reshape(held.shape)
    gain = jnp.broadcast_to(gain_ref[...], (LANES, LANES)).T
    for j in range(24):
        tri = held[pl.ds(j, LANES, stride=24), :]
        mean = jnp.mean(tri, axis=0, keepdims=True)
        centred = tri - mean
        var = jnp.mean(centred * centred, axis=0, keepdims=True)
        normed = (centred * lax.rsqrt(var + 1e-05) * gain).astype(BF16)
        projected = lax.dot_general(
            normed, wout_ref[...], (((0,), (0,)), ((), ())), preferred_element_type=F32
        )
        for bit in range(2):
            result[pl.ds(bit * 24 + j, 64, stride=48), :] = projected[bit * 64 : bit * 64 + 64]
    for part in range(24):
        rows = slice(part * LANES, part * LANES + LANES)
        out_ref[rows, :] = (gate_ref[rows, :] * result[rows, :]).astype(BF16)


def shape(dims, kind):
    return jax.ShapeDtypeStruct(dims, kind)


def exchange(values):
    return lax.all_to_all(values, CHIPS, split_axis=0, concat_axis=0, tiled=True)


def shards(z_band, z_square, ln_in_gain, w_a_gate, w_a, w_b_gate, w_b, w_g, ln_out_gain, w_out):
    gain_in = ln_in_gain.reshape(1, LANES)
    gain_out = ln_out_gain.reshape(1, LANES)
    rows = z_band.shape[0] * z_band.shape[1]
    band = z_band.reshape(rows, LANES)
    vmem = pl.BlockSpec(memory_space=pltpu.VMEM)
    hbm = pl.BlockSpec(memory_space=pltpu.HBM)
    edges = pl.pallas_call(
        edges_kernel,
        out_shape=pltpu.VMEM((LANES * MESSAGE, LANES), BF16),
        in_specs=[hbm] * 7,
        out_specs=vmem,
        scratch_shapes=[
            pltpu.VMEM((rows, LANES), BF16),
            pltpu.VMEM(z_square.shape, BF16),
            pltpu.VMEM((1, LANES), F32),
            pltpu.VMEM((4, LANES, LANES), BF16),
            pltpu.VMEM((rows, LANES), F32),
            pltpu.VMEM((LANES * MESSAGE, LANES), F32),
            pltpu.SemaphoreType.DMA((10,)),
        ],
        compiler_params=params(),
        name="edges",
    )(*[
        pltpu.with_memory_space_constraint(a, pltpu.HBM)
        for a in (band, z_square, gain_in, w_a_gate, w_a, w_b_gate, w_b)
    ])
    core = lax.axis_index("core").astype(jnp.int32).reshape(1)
    edges, core = lax.optimization_barrier((edges, core))
    edges = exchange(edges.reshape(LANES, MESSAGE // 2, 2, LANES)).reshape(edges.shape)
    own, other = pl.pallas_call(
        product_kernel,
        out_shape=(shape((384, 1024), F32), shape((384, 1024), BF16)),
        in_specs=[pl.BlockSpec(memory_space=pltpu.SMEM), vmem],
        out_specs=(vmem, vmem),
        scratch_shapes=[
            pltpu.VMEM((4, 384, 256), BF16),
            pltpu.VMEM((2, 384, 384), BF16),
            pltpu.VMEM((32 * MESSAGE + 8, LANES), F32),
            pltpu.VMEM((4, 8 * 24, LANES), F32),
        ],
        compiler_params=params(),
        name="product",
    )(core, edges)
    other, band, gain_in, w_g, gain_out, w_out = lax.optimization_barrier(
        (other, band, gain_in, w_g, gain_out, w_out)
    )
    other = lax.ppermute(other, "core", ((0, 1), (1, 0)))
    gate = pl.pallas_call(
        gate_kernel,
        out_shape=shape((rows, LANES), F32),
        compiler_params=params(),
        name="gate",
    )(band, gain_in, w_g)
    triangle = pl.pallas_call(
        sum_kernel,
        out_shape=pltpu.VMEM((LANES, 24, LANES), BF16),
        compiler_params=params(),
        name="sum",
    )(own, other)
    triangle, gate, gain_out = lax.optimization_barrier((triangle, gate, gain_out))
    triangle = exchange(triangle)
    update = pl.pallas_call(
        update_kernel,
        out_shape=shape((rows, LANES), BF16),
        scratch_shapes=[pltpu.VMEM((LANES * 24, LANES), F32), pltpu.VMEM((rows, LANES), F32)],
        compiler_params=params(),
        name="update",
    )(triangle, gate, gain_out, w_out)
    return update.reshape(z_band.shape)


def solution(mesh):
    names = tuple(name for name, _ in PARTS)
    fine = Mesh(mesh.devices.reshape(tuple(size for _, size in PARTS)), names)
    pair = P(("z", "y_lo"), ("x", "y_hi", "core"), None)
    placed = (pair, pair, P(), P(), P(), P(), P(), P(), P(), P())
    return jax.shard_map(
        shards, mesh=fine, in_specs=placed, out_specs=pair, check_vma=False
    )
```

profile of v0, /device:TPU:8, one launch (start us, length us, event | category | flops | bytes accessed | tf_op | source)
XLA Modules:
  0.0 96.8 jit_solution(17682879549028797614)
XLA Ops:
  0.0 4.1 %edges.1 = bf16[5376,128]{1,0:T(8,128)(2,1)S(1)} custom-call(bf16[3072,128]{1,0:T(8,128)(2,1)} %bitcast.9, bf16[48,48,128]{2,1,0:T(8,128)(2,1)} %square_hbm.1, f32[1,128]{1,0:T(1,128)} %bitcast.11, bf16[128,128]{1,0:T(8,128)(2,1)} %wag_hbm.1, bf16[128,128]{1,0:T(8,128)(2,1)} %wa_hbm.1, bf16[128,128]{1,0:T(8,128)(2,1)} %wbg_hbm.1, bf16[128,128]{1,0:T(8,128)(2,1)} %wb_hbm.1), custom_call_target="tpu_custom_call" | custom-call | tf_op jit(solution)/shard_map/edges/pallas_call | solution.py:222
  4.1 0.0 copy-start
  4.1 0.0 copy-start.2
  4.1 0.0 copy-start.3
  4.1 52.9 %all_to_all.10 = bf16[128,21,2,128]{3,2,1,0:T(2,128)(2,1)S(1)} all-to-all(bf16[128,21,2,128]{3,2,1,0:T(2,128)(2,1)S(1)} %bitcast.8), channel_id=1, replica_groups=mesh['z'=8,'y_lo'=2,'x'=4,'y_hi'=2,'core'=2] {'z','y_lo','x','y_hi'}, dimensions={0} | all-to-all | bytes 2752512 | tf_op jit(solution)/shard_map/all_to_all | solution.py:212
  57.0 3.1 %product.1 = (f32[384,1024]{1,0:T(8,128)S(1)}, bf16[384,1024]{1,0:T(8,128)(2,1)S(1)}) custom-call(s32[1]{0:T(128)} %bitcast.2.core_ref, bf16[5376,128]{1,0:T(8,128)(2,1)S(1)} %bitcast.7), custom_call_target="tpu_custom_call" | custom-call | tf_op jit(solution)/shard_map/product/pallas_call | solution.py:245
  60.1 0.1 collective-permute-start
  60.2 0.0 copy-done
  60.2 0.0 copy-done.2
  60.2 0.0 copy-done.3
  60.2 1.1 %gate.1.gate_ref = f32[3072,128]{1,0:T(8,128)S(1)} custom-call(bf16[3072,128]{1,0:T(8,128)(2,1)S(1)} %bitcast.10, f32[1,128]{1,0:T(1,128)S(1)} %bitcast.12, bf16[128,128]{1,0:T(8,128)(2,1)S(1)} %copy-done.2), custom_call_target="tpu_custom_call" | custom-call | tf_op jit(solution)/shard_map/gate/pallas_call | solution.py:263
  61.3 1.1 %collective-permute-done.other_ref = bf16[384,1024]{1,0:T(8,128)(2,1)S(1)} collective-permute-done((bf16[384,1024]{1,0:T(8,128)(2,1)S(1)}, bf16[384,1024]{1,0:T(8,128)(2,1)S(1)}, u32[]{:S(2)}, u32[]{:S(2)}) %collective-permute-start) | collective-permute-done | bytes 786464 | tf_op jit(solution)/shard_map/ppermute | solution.py:262
  62.5 0.3 sum.1
  62.8 0.0 copy-start.1
  62.8 0.0 copy-start.4
  62.8 31.7 %all_to_all.11.in_ref = bf16[128,24,128]{2,1,0:T(8,128)(2,1)S(1)} all-to-all(bf16[128,24,128]{2,1,0:T(8,128)(2,1)S(1)} %sum.1), channel_id=1, replica_groups=mesh['z'=8,'y_lo'=2,'x'=4,'y_hi'=2,'core'=2] {'z','y_lo','x','y_hi'}, dimensions={0} | all-to-all | bytes 1572864 | tf_op jit(solution)/shard_map/all_to_all | solution.py:212
  94.5 0.0 copy-done.1
  94.5 0.0 copy-done.4
  94.5 2.3 %update.1 = bf16[3072,128]{1,0:T(8,128)(2,1)} custom-call(bf16[128,24,128]{2,1,0:T(8,128)(2,1)S(1)} %all_to_all.11.in_ref, f32[3072,128]{1,0:T(8,128)S(1)} %gate.1.gate_ref, f32[1,128]{1,0:T(1,128)S(1)} %bitcast.13, bf16[128,128]{1,0:T(8,128)(2,1)S(1)} %copy-done.1), custom_call_target="tpu_custom_call" | custom-call | tf_op jit(solution)/shard_map/update/pallas_call | solution.py:277
Async XLA Ops:
  4.1 56.1 %copy-start = (bf16[64,48,128]{2,1,0:T(8,128)(2,1)S(1)}, bf16[64,48,128]{2,1,0:T(8,128)(2,1)}, u32[]{:S(2)}) copy-start(bf16[64,48,128]{2,1,0:T(8,128)(2,1)} %param.10) | copy-start | bytes 2359300
  4.1 56.1 %copy-start.2 = (bf16[128,128]{1,0:T(8,128)(2,1)S(1)}, bf16[128,128]{1,0:T(8,128)(2,1)}, u32[]{:S(2)}) copy-start(bf16[128,128]{1,0:T(8,128)(2,1)} %wg_ref) | copy-start | bytes 98308
  4.1 56.1 %copy-start.3 = (f32[128]{0:T(128)S(1)}, f32[128]{0:T(128)}, u32[]{:S(2)}) copy-start(f32[128]{0:T(128)} %param.12) | copy-start | bytes 1540
  60.1 2.4 %collective-permute-start = (bf16[384,1024]{1,0:T(8,128)(2,1)S(1)}, bf16[384,1024]{1,0:T(8,128)(2,1)S(1)}, u32[]{:S(2)}, u32[]{:S(2)}) collective-permute-start(bf16[384,1024]{1,0:T(8,128)(2,1)S(1)} %get-tuple-element.22), channel_id=1, source_target_pairs={{0,1},{1,0},{2,3},{3,2},{4,5},{5,4},{6,7},{7,6},{8,9},{9,8},{10,11... | collective-permute-start | bytes 2359304 | tf_op jit(solution)/shard_map/ppermute | solution.py:262
  62.8 31.7 %copy-start.1 = (bf16[128,128]{1,0:T(8,128)(2,1)S(1)}, bf16[128,128]{1,0:T(8,128)(2,1)}, u32[]{:S(2)}) copy-start(bf16[128,128]{1,0:T(8,128)(2,1)} %wout_ref) | copy-start | bytes 98308
  62.8 31.7 %copy-start.4 = (f32[128]{0:T(128)S(1)}, f32[128]{0:T(128)}, u32[]{:S(2)}) copy-start(f32[128]{0:T(128)} %param.18) | copy-start | bytes 1540
where the time goes:
time: 97 us; the launch traced here: 96.8 us
  blocking collectives  84.6 us (87%)
  Pallas kernels  10.8 us (11%)
  waiting for transfers between devices  1.14 us (1%)
    all_to_all x2, blocking collectives, exchange(): lax.all_to_all(values, CHIPS, split_axis=0, concat_axis=0, tiled=True)  84.6 us
    pallas_call x1, Pallas kernels, shards(): pl.pallas_call(edges_kernel, out_shape=pltpu.VMEM((LANES * MESSAGE, LANES...  4.1 us
    pallas_call x1, Pallas kernels, shards(): pl.pallas_call(product_kernel, out_shape=(shape((384, 1024), F32), shape(...  3.06 us
    pallas_call x1, Pallas kernels, shards(): pl.pallas_call(update_kernel, out_shape=shape((rows, LANES), BF16), scrat...  2.27 us
  transfers between devices with their start and end apart: 1, of which 1 were waited for; matrix products, arithmetic and copies ran while one was open for 0% of the time, Pallas kernels for 1%

commit v1 on v0

--- a/solution.py
+++ b/solution.py
@@ -15,6 +15,7 @@
 COLS = 8
 LANES = 128
 MESSAGE = 42
+PITCH = 25
 VMEM = 40 * 1024 * 1024
 
 
@@ -41,8 +42,11 @@
                 continue
             second = first | (1 << bit)
             a, b = arrays[first], arrays[second]
-            arrays[first] = jnp.where(low, a, pltpu.roll(b, shift, axis))
-            arrays[second] = jnp.where(low, pltpu.roll(a, LANES - shift, axis), b)
+            if 2 * shift == LANES:
+                up = down = pltpu.roll(jnp.where(low, b, a), shift, axis)
+            else:
+                up, down = pltpu.roll(b, shift, axis), pltpu.roll(a, LANES - shift, axis)
+            arrays[first], arrays[second] = jnp.where(low, a, up), jnp.where(low, down, b)
     return arrays
 
 
@@ -78,8 +82,7 @@
         rows = slice(part * LANES, part * LANES + LANES)
         z = band[rows, :]
         centred = z.astype(F32) - jnp.dot(z, share, preferred_element_type=F32)
-        squares = (centred * centred).astype(BF16)
-        var = jnp.dot(squares, share, preferred_element_type=F32)
+        var = jnp.mean(centred * centred, axis=-1, keepdims=True)
         normed[rows, :] = centred * lax.rsqrt(var + 1e-05) * gain
     for copy in copies[5:]:
         copy.wait()
@@ -114,7 +117,7 @@
     return jnp.where(low, a, moved), jnp.where(low, moved, b)
 
 
-def product_kernel(core_ref, in_ref, own_ref, other_ref, left, right, raw, held):
+def product_kernel(core_ref, in_ref, other_ref, left, right, raw, held):
     size = 32 * MESSAGE
 
     def quad(p, carry):
@@ -134,16 +137,24 @@
                         k3 * LANES + q * 16 : k3 * LANES + q * 16 + 16,
                         half * LANES : half * LANES + LANES,
                     ] = jnp.concatenate(blocks[2 * k3 : 2 * k3 + 2], axis=0).astype(BF16)
-        for n in range(4):
+        for half in range(2):
             for k3 in range(3):
-                blocks = swap([rows(n * 8 + q, 24 + k3) for q in range(8)])
+                blocks = swap([
+                    jnp.concatenate(
+                        [rows(half * 16 + odd * 8 + q, 24 + k3) for odd in range(2)], axis=0
+                    ).astype(BF16)
+                    for q in range(8)
+                ])
                 for lo in range(8):
-                    held[n, lo * 24 + k3 * 8 : lo * 24 + k3 * 8 + 8, :] = blocks[lo]
+                    block = blocks[lo].astype(F32)
+                    start = lo * PITCH + k3 * 8
+                    for odd in range(2):
+                        held[half * 2 + odd, start : start + 8, :] = block[odd * 8 : odd * 8 + 8]
         for core in range(2):
             for k3 in range(3):
                 for hi in range(6):
                     tiles = [
-                        held[half * 2 + core, pl.ds(k3 * 8 + hi, 8, stride=24), :]
+                        held[half * 2 + core, pl.ds(k3 * 8 + hi, 8, stride=PITCH), :]
                         for half in range(2)
                     ]
                     right[
@@ -154,12 +165,18 @@
         return carry
 
     lax.fori_loop(0, 4, quad, 0)
-    core = core_ref[0]
-    for which, ref in ((1 - core, other_ref), (core, own_ref)):
-        for p in range(4):
-            ref[:, p * 256 : p * 256 + 256] = jnp.dot(
-                right[which], left[p], preferred_element_type=F32
-            ).astype(ref.dtype)
+    multiply(right, left, 1 - core_ref[0], other_ref)
+
+
+def multiply(right, left, core, out_ref):
+    for p in range(4):
+        out_ref[:, p * 256 : p * 256 + 256] = jnp.dot(
+            right[core], left[p], preferred_element_type=F32
+        ).astype(out_ref.dtype)
+
+
+def own_kernel(core_ref, left, right, own_ref):
+    multiply(right, left, core_ref[0], own_ref)
 
 
 def sum_kernel(own_ref, other_ref, out_ref):
@@ -186,10 +203,11 @@
 
 
 def update_kernel(in_ref, gate_ref, gain_ref, wout_ref, out_ref, held, result):
-    held[...] = in_ref[...].astype(F32).reshape(held.shape)
+    for h in range(LANES):
+        held[h * PITCH : h * PITCH + 24, :] = in_ref[h].astype(F32)
     gain = jnp.broadcast_to(gain_ref[...], (LANES, LANES)).T
     for j in range(24):
-        tri = held[pl.ds(j, LANES, stride=24), :]
+        tri = held[pl.ds(j, LANES, stride=PITCH), :]
         mean = jnp.mean(tri, axis=0, keepdims=True)
         centred = tri - mean
         var = jnp.mean(centred * centred, axis=0, keepdims=True)
@@ -198,10 +216,10 @@
             normed, wout_ref[...], (((0,), (0,)), ((), ())), preferred_element_type=F32
         )
         for bit in range(2):
-            result[pl.ds(bit * 24 + j, 64, stride=48), :] = projected[bit * 64 : bit * 64 + 64]
-    for part in range(24):
-        rows = slice(part * LANES, part * LANES + LANES)
-        out_ref[rows, :] = (gate_ref[rows, :] * result[rows, :]).astype(BF16)
+            result[pl.ds(bit * 24 + j, 64, stride=49), :] = projected[bit * 64 : bit * 64 + 64]
+    for i in range(64):
+        rows = slice(i * 48, i * 48 + 48)
+        out_ref[rows, :] = (gate_ref[rows, :] * result[i * 49 : i * 49 + 48, :]).astype(BF16)
 
 
 def shape(dims, kind):
@@ -242,16 +260,19 @@
     core = lax.axis_index("core").astype(jnp.int32).reshape(1)
     edges, core = lax.optimization_barrier((edges, core))
     edges = exchange(edges.reshape(LANES, MESSAGE // 2, 2, LANES)).reshape(edges.shape)
-    own, other = pl.pallas_call(
+    smem = pl.BlockSpec(memory_space=pltpu.SMEM)
+    other, left, right = pl.pallas_call(
         product_kernel,
-        out_shape=(shape((384, 1024), F32), shape((384, 1024), BF16)),
-        in_specs=[pl.BlockSpec(memory_space=pltpu.SMEM), vmem],
-        out_specs=(vmem, vmem),
-        scratch_shapes=[
+        out_shape=(
+            pltpu.VMEM((384, 1024), BF16),
             pltpu.VMEM((4, 384, 256), BF16),
             pltpu.VMEM((2, 384, 384), BF16),
+        ),
+        in_specs=[smem, vmem],
+        out_specs=(vmem, vmem, vmem),
+        scratch_shapes=[
             pltpu.VMEM((32 * MESSAGE + 8, LANES), F32),
-            pltpu.VMEM((4, 8 * 24, LANES), F32),
+            pltpu.VMEM((4, 8 * PITCH + 8, LANES), F32),
         ],
         compiler_params=params(),
         name="product",
@@ -260,6 +281,14 @@
         (other, band, gain_in, w_g, gain_out, w_out)
     )
     other = lax.ppermute(other, "core", ((0, 1), (1, 0)))
+    own = pl.pallas_call(
+        own_kernel,
+        out_shape=pltpu.VMEM((384, 1024), F32),
+        in_specs=[smem, vmem, vmem],
+        out_specs=vmem,
+        compiler_params=params(),
+        name="own",
+    )(core, left, right)
     gate = pl.pallas_call(
         gate_kernel,
         out_shape=shape((rows, LANES), F32),
@@ -277,7 +306,7 @@
     update = pl.pallas_call(
         update_kernel,
         out_shape=shape((rows, LANES), BF16),
-        scratch_shapes=[pltpu.VMEM((LANES * 24, LANES), F32), pltpu.VMEM((rows, LANES), F32)],
+        scratch_shapes=[pltpu.VMEM((LANES * PITCH, LANES), F32), pltpu.VMEM((64 * 49, LANES), F32)],
         compiler_params=params(),
         name="update",
     )(triangle, gate, gain_out, w_out)

time: 97 us -> 95.1 us (0.980)
  Pallas kernels: 10.8 us -> 9.65 us
  waiting for transfers between devices: 1.14 us -> 0.14 us
    ppermute x1, waiting for transfers between devices: 1.14 us -> 0.14 us  [shards(): other = lax.ppermute(other, 'core', ((0, 1), (1, 0)))]
    pallas_call x1 -> x2, Pallas kernels: 3.06 us -> 2.56 us  [the longest x1 1.99 us: shards(): pl.pallas_call(product_kernel, out_shape=(pltpu.VMEM((384, 1024), BF16),...]
  transfers between devices with their start and end apart: 1 -> 1, of which waited for: 1 -> 1; matrix products, arithmetic and copies ran while one was open for 0% -> 0% of each run, Pallas kernels for 1% -> 2%
where the time goes in v1:
time: 95.1 us; the launch traced here: 94.9 us
  blocking collectives  84.5 us (89%)
  Pallas kernels  9.65 us (10%)
    all_to_all x2, blocking collectives, exchange(): lax.all_to_all(values, CHIPS, split_axis=0, concat_axis=0, tiled=True)  84.5 us
    pallas_call x1, Pallas kernels, shards(): pl.pallas_call(edges_kernel, out_shape=pltpu.VMEM((LANES * MESSAGE, LANES...  3.98 us
    pallas_call x1, Pallas kernels, shards(): pl.pallas_call(product_kernel, out_shape=(pltpu.VMEM((384, 1024), BF16),...  1.99 us
  transfers between devices with their start and end apart: 1, of which 1 were waited for; matrix products, arithmetic and copies ran while one was open for 0% of the time, Pallas kernels for 2%

profile of v1, /device:TPU:8, one launch (start us, length us, event | category | flops | bytes accessed | tf_op | source)
XLA Modules:
  0.0 94.9 jit_solution(2606115829693617545)
XLA Ops:
  0.0 4.0 %edges.1 = bf16[5376,128]{1,0:T(8,128)(2,1)S(1)} custom-call(bf16[3072,128]{1,0:T(8,128)(2,1)} %bitcast.9, bf16[48,48,128]{2,1,0:T(8,128)(2,1)} %square_hbm.1, f32[1,128]{1,0:T(1,128)} %bitcast.11, bf16[128,128]{1,0:T(8,128)(2,1)} %wag_hbm.1, bf16[128,128]{1,0:T(8,128)(2,1)} %wa_hbm.1, bf16[128,128]{1,0:T(8,128)(2,1)} %wbg_hbm.1, bf16[128,128]{1,0:T(8,128)(2,1)} %wb_hbm.1), custom_call_target="tpu_custom_call" | custom-call | tf_op jit(solution)/shard_map/edges/pallas_call | solution.py:240
  4.0 52.8 %all_to_all.10 = bf16[128,21,2,128]{3,2,1,0:T(2,128)(2,1)S(1)} all-to-all(bf16[128,21,2,128]{3,2,1,0:T(2,128)(2,1)S(1)} %bitcast.8), channel_id=1, replica_groups=mesh['z'=8,'y_lo'=2,'x'=4,'y_hi'=2,'core'=2] {'z','y_lo','x','y_hi'}, dimensions={0} | all-to-all | bytes 2752512 | tf_op jit(solution)/shard_map/all_to_all | solution.py:230
  56.7 2.0 %product.1 = (bf16[384,1024]{1,0:T(8,128)(2,1)S(1)}, bf16[4,384,256]{2,1,0:T(8,128)(2,1)S(1)}, bf16[2,384,384]{2,1,0:T(8,128)(2,1)S(1)}) custom-call(s32[1]{0:T(128)} %bitcast.2.core_ref, bf16[5376,128]{1,0:T(8,128)(2,1)S(1)} %bitcast.7), custom_call_target="tpu_custom_call" | custom-call | tf_op jit(solution)/shard_map/product/pallas_call | solution.py:264
  58.7 0.0 copy-start
  58.7 0.0 copy-start.2
  58.8 0.0 copy-start.3
  58.8 0.1 collective-permute-start
  58.9 0.6 own.1.own_ref
  59.4 0.4 copy-done
  59.9 0.0 copy-done.2
  59.9 0.0 copy-done.3
  59.9 1.1 %gate.1.gate_ref = f32[3072,128]{1,0:T(8,128)S(1)} custom-call(bf16[3072,128]{1,0:T(8,128)(2,1)S(1)} %bitcast.10, f32[1,128]{1,0:T(1,128)S(1)} %bitcast.12, bf16[128,128]{1,0:T(8,128)(2,1)S(1)} %copy-done.2), custom_call_target="tpu_custom_call" | custom-call | tf_op jit(solution)/shard_map/gate/pallas_call | solution.py:292
  61.0 0.0 copy-start.1
  61.0 0.0 copy-start.4
  61.0 0.1 collective-permute-done.other_ref
  61.1 0.3 sum.1
  61.5 31.7 %all_to_all.11.in_ref = bf16[128,24,128]{2,1,0:T(8,128)(2,1)S(1)} all-to-all(bf16[128,24,128]{2,1,0:T(8,128)(2,1)S(1)} %sum.1), channel_id=1, replica_groups=mesh['z'=8,'y_lo'=2,'x'=4,'y_hi'=2,'core'=2] {'z','y_lo','x','y_hi'}, dimensions={0} | all-to-all | bytes 1572864 | tf_op jit(solution)/shard_map/all_to_all | solution.py:230
  93.2 0.0 copy-done.1
  93.2 0.0 copy-done.4
  93.2 1.7 %update.1 = bf16[3072,128]{1,0:T(8,128)(2,1)} custom-call(bf16[128,24,128]{2,1,0:T(8,128)(2,1)S(1)} %all_to_all.11.in_ref, f32[3072,128]{1,0:T(8,128)S(1)} %gate.1.gate_ref, f32[1,128]{1,0:T(1,128)S(1)} %bitcast.13, bf16[128,128]{1,0:T(8,128)(2,1)S(1)} %copy-done.1), custom_call_target="tpu_custom_call" | custom-call | tf_op jit(solution)/shard_map/update/pallas_call | solution.py:306
Async XLA Ops:
  58.7 1.1 %copy-start = (bf16[64,48,128]{2,1,0:T(8,128)(2,1)S(1)}, bf16[64,48,128]{2,1,0:T(8,128)(2,1)}, u32[]{:S(2)}) copy-start(bf16[64,48,128]{2,1,0:T(8,128)(2,1)} %param.10) | copy-start | bytes 2359300
  58.7 1.1 %copy-start.2 = (bf16[128,128]{1,0:T(8,128)(2,1)S(1)}, bf16[128,128]{1,0:T(8,128)(2,1)}, u32[]{:S(2)}) copy-start(bf16[128,128]{1,0:T(8,128)(2,1)} %wg_ref) | copy-start | bytes 98308
  58.8 1.1 %copy-start.3 = (f32[128]{0:T(128)S(1)}, f32[128]{0:T(128)}, u32[]{:S(2)}) copy-start(f32[128]{0:T(128)} %param.12) | copy-start | bytes 1540
  58.8 2.4 %collective-permute-start = (bf16[384,1024]{1,0:T(8,128)(2,1)S(1)}, bf16[384,1024]{1,0:T(8,128)(2,1)S(1)}, u32[]{:S(2)}, u32[]{:S(2)}) collective-permute-start(bf16[384,1024]{1,0:T(8,128)(2,1)S(1)} %get-tuple-element.24), channel_id=1, source_target_pairs={{0,1},{1,0},{2,3},{3,2},{4,5},{5,4},{6,7},{7,6},{8,9},{9,8},{10,11... | collective-permute-start | bytes 2359304 | tf_op jit(solution)/shard_map/ppermute | solution.py:283
  61.0 32.2 %copy-start.1 = (bf16[128,128]{1,0:T(8,128)(2,1)S(1)}, bf16[128,128]{1,0:T(8,128)(2,1)}, u32[]{:S(2)}) copy-start(bf16[128,128]{1,0:T(8,128)(2,1)} %wout_ref) | copy-start | bytes 98308
  61.0 32.2 %copy-start.4 = (f32[128]{0:T(128)S(1)}, f32[128]{0:T(128)}, u32[]{:S(2)}) copy-start(f32[128]{0:T(128)} %param.18) | copy-start | bytes 1540

commit v2 on v1

--- a/solution.py
+++ b/solution.py
@@ -21,13 +21,6 @@
 
 def params():
     return pltpu.CompilerParams(vmem_limit_bytes=VMEM)
-
-
-def layer_norm(values, gain):
-    mean = jnp.mean(values, axis=-1, keepdims=True)
-    centred = values - mean
-    var = jnp.mean(centred * centred, axis=-1, keepdims=True)
-    return centred * lax.rsqrt(var + 1e-05) * gain
 
 
 def swap(arrays):
@@ -51,8 +44,8 @@
 
 
 def edges_kernel(
-    band_hbm, square_hbm, gain_hbm, wag_hbm, wa_hbm, wbg_hbm, wb_hbm, out_ref,
-    band, square, gain_ref, weights, normed, held, sems,
+    band_hbm, square_hbm, gain_hbm, wag_hbm, wa_hbm, wbg_hbm, wb_hbm, out_ref, band_norm,
+    band, square, gain_ref, weights, normed, square_norm, held, sems,
 ):
     quarter = band.shape[0] // 4
     parts = [slice(n * quarter, n * quarter + quarter) for n in range(4)]
@@ -76,16 +69,24 @@
         both = lax.dot_general(both, rows, (((1,), (1,)), ((), ())), preferred_element_type=F32)
         return jax.nn.sigmoid(both[:LANES]) * both[LANES:]
 
+    def normalise(z):
+        centred = z.astype(F32) - jnp.dot(z, share, preferred_element_type=F32)
+        var = jnp.mean(centred * centred, axis=-1, keepdims=True)
+        return centred * lax.rsqrt(var + 1e-05) * gain
+
     for part in range(24):
         if part % 6 == 0:
             copies[1 + part // 6].wait()
         rows = slice(part * LANES, part * LANES + LANES)
-        z = band[rows, :]
-        centred = z.astype(F32) - jnp.dot(z, share, preferred_element_type=F32)
-        var = jnp.mean(centred * centred, axis=-1, keepdims=True)
-        normed[rows, :] = centred * lax.rsqrt(var + 1e-05) * gain
+        norm = normalise(band[rows, :])
+        normed[rows, :] = norm
+        band_norm[rows, :] = norm.astype(BF16)
     for copy in copies[5:]:
         copy.wait()
+    for step in range(9):
+        k3, hi = step // 3, step % 3 * 2
+        z = square[hi * 8 : hi * 8 + 16, k3 * 16 : k3 * 16 + 16, :].reshape(2 * LANES, LANES)
+        square_norm[step] = normalise(z).astype(BF16)
     left = jnp.concatenate([weights[0].T, weights[1].T], axis=0)
     right = jnp.concatenate([weights[2].T, weights[3].T], axis=0)
     for step in range(12):
@@ -102,8 +103,7 @@
             ]
         if step < 9:
             k3, hi = step // 3, step % 3 * 2
-            z = square[hi * 8 : hi * 8 + 16, k3 * 16 : k3 * 16 + 16, :].reshape(2 * LANES, LANES)
-            edge = project(right, layer_norm(z.astype(F32), gain).astype(BF16))
+            edge = project(right, square_norm[step])
             for odd in range(2):
                 held[pl.ds(24 + (hi + odd) * 3 + k3, LANES, stride=MESSAGE), :] = edge[
                     :, odd * LANES : odd * LANES + LANES
@@ -117,14 +117,44 @@
     return jnp.where(low, a, moved), jnp.where(low, moved, b)
 
 
+def arrange_right(rows, right, held, p):
+    for k3 in range(3):
+        blocks = swap([
+            jnp.concatenate([rows(half, q, k3) for half in range(2)], axis=0).astype(BF16)
+            for q in range(8)
+        ])
+        for lo in range(8):
+            block = blocks[lo].astype(F32)
+            start = lo * PITCH + k3 * 8
+            for half in range(2):
+                held[half, start : start + 8, :] = block[half * 8 : half * 8 + 8]
+    for k3 in range(3):
+        for hi in range(6):
+            tiles = [held[half, pl.ds(k3 * 8 + hi, 8, stride=PITCH), :] for half in range(2)]
+            right[
+                hi * 64 + p * 16 : hi * 64 + p * 16 + 16, k3 * LANES : k3 * LANES + LANES
+            ] = jnp.concatenate(tiles, axis=0).astype(BF16)
+
+
+def multiply(right, left, out_ref):
+    for p in range(4):
+        out_ref[:, p * 256 : p * 256 + 256] = jnp.dot(
+            right[...], left[p], preferred_element_type=F32
+        ).astype(out_ref.dtype)
+
+
 def product_kernel(core_ref, in_ref, other_ref, left, right, raw, held):
     size = 32 * MESSAGE
-
-    def quad(p, carry):
-        raw[:size, :] = in_ref[pl.ds(pl.multiple_of(p * size, 16), size), :].astype(F32)
-
-        def rows(n, start):
-            return raw[pl.ds(n * MESSAGE + start, 8, stride=3), :]
+    there = pl.multiple_of((1 - core_ref[0]) * (8 * MESSAGE), 8)
+
+    for p in range(4):
+        raw[p, :size, :] = in_ref[p * size : p * size + size, :].astype(F32)
+
+        def rows(n, kb, p=p):
+            return raw[p, pl.ds(n * MESSAGE + kb, 8, stride=3), :]
+
+        def right_rows(half, q, k3, p=p):
+            return raw[p, pl.ds(there + ((half * 16 + q) * MESSAGE + 24 + k3), 8, stride=3), :]
 
         for half in range(2):
             for q in range(8):
@@ -137,46 +167,24 @@
                         k3 * LANES + q * 16 : k3 * LANES + q * 16 + 16,
                         half * LANES : half * LANES + LANES,
                     ] = jnp.concatenate(blocks[2 * k3 : 2 * k3 + 2], axis=0).astype(BF16)
+        arrange_right(right_rows, right, held.at[p], p)
+    multiply(right, left, other_ref)
+
+
+def own_kernel(core_ref, in_ref, left, own_ref, right, raw, held):
+    size = 8 * MESSAGE
+    here = core_ref[0] * size
+
+    for p in range(4):
         for half in range(2):
-            for k3 in range(3):
-                blocks = swap([
-                    jnp.concatenate(
-                        [rows(half * 16 + odd * 8 + q, 24 + k3) for odd in range(2)], axis=0
-                    ).astype(BF16)
-                    for q in range(8)
-                ])
-                for lo in range(8):
-                    block = blocks[lo].astype(F32)
-                    start = lo * PITCH + k3 * 8
-                    for odd in range(2):
-                        held[half * 2 + odd, start : start + 8, :] = block[odd * 8 : odd * 8 + 8]
-        for core in range(2):
-            for k3 in range(3):
-                for hi in range(6):
-                    tiles = [
-                        held[half * 2 + core, pl.ds(k3 * 8 + hi, 8, stride=PITCH), :]
-                        for half in range(2)
-                    ]
-                    right[
-                        core,
-                        pl.ds(pl.multiple_of(hi * 64 + p * 16, 16), 16),
-                        k3 * LANES : k3 * LANES + LANES,
-                    ] = jnp.concatenate(tiles, axis=0).astype(BF16)
-        return carry
-
-    lax.fori_loop(0, 4, quad, 0)
-    multiply(right, left, 1 - core_ref[0], other_ref)
-
-
-def multiply(right, left, core, out_ref):
-    for p in range(4):
-        out_ref[:, p * 256 : p * 256 + 256] = jnp.dot(
-            right[core], left[p], preferred_element_type=F32
-        ).astype(out_ref.dtype)
-
-
-def own_kernel(core_ref, left, right, own_ref):
-    multiply(right, left, core_ref[0], own_ref)
+            start = pl.multiple_of((p * 4 + half * 2) * size + here, 16)
+            raw[p, half * size : half * size + size, :] = in_ref[pl.ds(start, size), :].astype(F32)
+
+        def right_rows(half, q, k3, p=p):
+            return raw[p, pl.ds((half * 8 + q) * MESSAGE + 24 + k3, 8, stride=3), :]
+
+        arrange_right(right_rows, right, held.at[p], p)
+    multiply(right, left, own_ref)
 
 
 def sum_kernel(own_ref, other_ref, out_ref):
@@ -197,9 +205,10 @@
                     ).astype(BF16)
 
 
-def gate_kernel(band_ref, gain_ref, wg_ref, out_ref):
-    normed = layer_norm(band_ref[...].astype(F32), gain_ref[...]).astype(BF16)
-    out_ref[...] = jax.nn.sigmoid(jnp.dot(normed, wg_ref[...], preferred_element_type=F32))
+def gate_kernel(norm_ref, wg_ref, out_ref):
+    out_ref[...] = jax.nn.sigmoid(
+        jnp.dot(norm_ref[...], wg_ref[...], preferred_element_type=F32)
+    )
 
 
 def update_kernel(in_ref, gate_ref, gain_ref, wout_ref, out_ref, held, result):
@@ -237,17 +246,21 @@
     band = z_band.reshape(rows, LANES)
     vmem = pl.BlockSpec(memory_space=pltpu.VMEM)
     hbm = pl.BlockSpec(memory_space=pltpu.HBM)
-    edges = pl.pallas_call(
+    edges, band_norm = pl.pallas_call(
         edges_kernel,
-        out_shape=pltpu.VMEM((LANES * MESSAGE, LANES), BF16),
+        out_shape=(
+            pltpu.VMEM((LANES * MESSAGE, LANES), BF16),
+            pltpu.VMEM((rows, LANES), BF16),
+        ),
         in_specs=[hbm] * 7,
-        out_specs=vmem,
+        out_specs=(vmem, vmem),
         scratch_shapes=[
             pltpu.VMEM((rows, LANES), BF16),
             pltpu.VMEM(z_square.shape, BF16),
             pltpu.VMEM((1, LANES), F32),
             pltpu.VMEM((4, LANES, LANES), BF16),
             pltpu.VMEM((rows, LANES), F32),
+            pltpu.VMEM((9, 2 * LANES, LANES), BF16),
             pltpu.VMEM((LANES * MESSAGE, LANES), F32),
             pltpu.SemaphoreType.DMA((10,)),
         ],
@@ -261,40 +274,40 @@
     edges, core = lax.optimization_barrier((edges, core))
     edges = exchange(edges.reshape(LANES, MESSAGE // 2, 2, LANES)).reshape(edges.shape)
     smem = pl.BlockSpec(memory_space=pltpu.SMEM)
-    other, left, right = pl.pallas_call(
+    other, left = pl.pallas_call(
         product_kernel,
-        out_shape=(
-            pltpu.VMEM((384, 1024), BF16),
-            pltpu.VMEM((4, 384, 256), BF16),
-            pltpu.VMEM((2, 384, 384), BF16),
-        ),
+        out_shape=(pltpu.VMEM((384, 1024), BF16), pltpu.VMEM((4, 384, 256), BF16)),
         in_specs=[smem, vmem],
-        out_specs=(vmem, vmem, vmem),
+        out_specs=(vmem, vmem),
         scratch_shapes=[
-            pltpu.VMEM((32 * MESSAGE + 8, LANES), F32),
-            pltpu.VMEM((4, 8 * PITCH + 8, LANES), F32),
+            pltpu.VMEM((384, 384), BF16),
+            pltpu.VMEM((4, 32 * MESSAGE + 8, LANES), F32),
+            pltpu.VMEM((4, 2, 8 * PITCH + 8, LANES), F32),
         ],
         compiler_params=params(),
         name="product",
     )(core, edges)
-    other, band, gain_in, w_g, gain_out, w_out = lax.optimization_barrier(
-        (other, band, gain_in, w_g, gain_out, w_out)
-    )
+    other, left, band_norm, gain_out = lax.optimization_barrier((other, left, band_norm, gain_out))
     other = lax.ppermute(other, "core", ((0, 1), (1, 0)))
     own = pl.pallas_call(
         own_kernel,
         out_shape=pltpu.VMEM((384, 1024), F32),
         in_specs=[smem, vmem, vmem],
         out_specs=vmem,
+        scratch_shapes=[
+            pltpu.VMEM((384, 384), BF16),
+            pltpu.VMEM((4, 16 * MESSAGE + 8, LANES), F32),
+            pltpu.VMEM((4, 2, 8 * PITCH + 8, LANES), F32),
+        ],
         compiler_params=params(),
         name="own",
-    )(core, left, right)
+    )(core, edges, left)
     gate = pl.pallas_call(
         gate_kernel,
         out_shape=shape((rows, LANES), F32),
         compiler_params=params(),
         name="gate",
-    )(band, gain_in, w_g)
+    )(band_norm, w_g)
     triangle = pl.pallas_call(
         sum_kernel,
         out_shape=pltpu.VMEM((LANES, 24, LANES), BF16),

time: 95.1 us -> 94.1 us (0.989)
  Pallas kernels: 9.65 us -> 8.43 us
  transfers between devices with their start and end apart: 1 -> 1, of which waited for: 1 -> 1; matrix products, arithmetic and copies ran while one was open for 0% -> 0% of each run, Pallas kernels for 2% -> 1%
where the time goes in v2:
time: 94.1 us; the launch traced here: 94 us
  blocking collectives  84.5 us (90%)
  Pallas kernels  8.43 us (9%)
    all_to_all x2, blocking collectives, exchange(): lax.all_to_all(values, CHIPS, split_axis=0, concat_axis=0, tiled=True)  84.5 us
    pallas_call x1, Pallas kernels, shards(): pl.pallas_call(edges_kernel, out_shape=(pltpu.VMEM((LANES * MESSAGE, LANE...  3.85 us
  transfers between devices with their start and end apart: 1, of which 1 were waited for; matrix products, arithmetic and copies ran while one was open for 0% of the time, Pallas kernels for 1%

profile of v2, /device:TPU:8, one launch (start us, length us, event | category | flops | bytes accessed | tf_op | source)
XLA Modules:
  0.0 94.0 jit_solution(13527318390275230532)
XLA Ops:
  0.0 3.9 %edges.1 = (bf16[5376,128]{1,0:T(8,128)(2,1)S(1)}, bf16[3072,128]{1,0:T(8,128)(2,1)S(1)}) custom-call(bf16[3072,128]{1,0:T(8,128)(2,1)} %bitcast.11, bf16[48,48,128]{2,1,0:T(8,128)(2,1)} %square_hbm.1, f32[1,128]{1,0:T(1,128)} %bitcast.12, bf16[128,128]{1,0:T(8,128)(2,1)} %wag_hbm.1, bf16[128,128]{1,0:T(8,128)(2,1)} %wa_hbm.1, bf16[128,128]{1,0:T(8,128)(2,1)} %wbg_hbm.1, ...), custom_call_target="tpu_custom_call" | custom-call | tf_op jit(solution)/shard_map/edges/pallas_call | solution.py:249
  3.9 52.8 %all_to_all.10 = bf16[128,21,2,128]{3,2,1,0:T(2,128)(2,1)S(1)} all-to-all(bf16[128,21,2,128]{3,2,1,0:T(2,128)(2,1)S(1)} %bitcast.9), channel_id=1, replica_groups=mesh['z'=8,'y_lo'=2,'x'=4,'y_hi'=2,'core'=2] {'z','y_lo','x','y_hi'}, dimensions={0} | all-to-all | bytes 2752512 | tf_op jit(solution)/shard_map/all_to_all | solution.py:239
  56.6 1.2 %product.1 = (bf16[384,1024]{1,0:T(8,128)(2,1)S(1)}, bf16[4,384,256]{2,1,0:T(8,128)(2,1)S(1)}) custom-call(s32[1]{0:T(128)} %bitcast.2.core_ref, bf16[5376,128]{1,0:T(8,128)(2,1)S(1)} %bitcast.7), custom_call_target="tpu_custom_call" | custom-call | tf_op jit(solution)/shard_map/product/pallas_call | solution.py:277
  57.9 0.0 copy-start
  57.9 0.1 collective-permute-start
  58.0 1.0 %own.1.own_ref = f32[384,1024]{1,0:T(8,128)S(1)} custom-call(s32[1]{0:T(128)} %bitcast.2.core_ref, bf16[5376,128]{1,0:T(8,128)(2,1)S(1)} %bitcast.8, bf16[4,384,256]{2,1,0:T(8,128)(2,1)S(1)} %get-tuple-element.24.left), custom_call_target="tpu_custom_call" | custom-call | tf_op jit(solution)/shard_map/own/pallas_call | solution.py:292
  58.9 0.0 copy-done
  58.9 0.4 gate.1.gate_ref
  59.3 0.0 copy-start.1
  59.3 0.0 copy-start.2
  59.3 0.9 collective-permute-done.other_ref
  60.2 0.3 sum.1
  60.6 31.7 %all_to_all.11.in_ref = bf16[128,24,128]{2,1,0:T(8,128)(2,1)S(1)} all-to-all(bf16[128,24,128]{2,1,0:T(8,128)(2,1)S(1)} %sum.1), channel_id=1, replica_groups=mesh['z'=8,'y_lo'=2,'x'=4,'y_hi'=2,'core'=2] {'z','y_lo','x','y_hi'}, dimensions={0} | all-to-all | bytes 1572864 | tf_op jit(solution)/shard_map/all_to_all | solution.py:239
  92.3 0.0 copy-done.1
  92.3 0.0 copy-done.2
  92.3 1.7 %update.1 = bf16[3072,128]{1,0:T(8,128)(2,1)} custom-call(bf16[128,24,128]{2,1,0:T(8,128)(2,1)S(1)} %all_to_all.11.in_ref, f32[3072,128]{1,0:T(8,128)S(1)} %gate.1.gate_ref, f32[1,128]{1,0:T(1,128)S(1)} %bitcast.10, bf16[128,128]{1,0:T(8,128)(2,1)S(1)} %copy-done.1), custom_call_target="tpu_custom_call" | custom-call | tf_op jit(solution)/shard_map/update/pallas_call | solution.py:319
Async XLA Ops:
  57.9 1.1 %copy-start = (bf16[128,128]{1,0:T(8,128)(2,1)S(1)}, bf16[128,128]{1,0:T(8,128)(2,1)}, u32[]{:S(2)}) copy-start(bf16[128,128]{1,0:T(8,128)(2,1)} %wg_ref.1) | copy-start | bytes 98308
  57.9 2.4 %collective-permute-start = (bf16[384,1024]{1,0:T(8,128)(2,1)S(1)}, bf16[384,1024]{1,0:T(8,128)(2,1)S(1)}, u32[]{:S(2)}, u32[]{:S(2)}) collective-permute-start(bf16[384,1024]{1,0:T(8,128)(2,1)S(1)} %get-tuple-element.25), channel_id=1, source_target_pairs={{0,1},{1,0},{2,3},{3,2},{4,5},{5,4},{6,7},{7,6},{8,9},{9,8},{10,11... | collective-permute-start | bytes 2359304 | tf_op jit(solution)/shard_map/ppermute | solution.py:291
  59.3 33.0 %copy-start.1 = (bf16[128,128]{1,0:T(8,128)(2,1)S(1)}, bf16[128,128]{1,0:T(8,128)(2,1)}, u32[]{:S(2)}) copy-start(bf16[128,128]{1,0:T(8,128)(2,1)} %wout_ref.1) | copy-start | bytes 98308
  59.3 33.0 %copy-start.2 = (f32[128]{0:T(128)S(1)}, f32[128]{0:T(128)}, u32[]{:S(2)}) copy-start(f32[128]{0:T(128)} %param.18) | copy-start | bytes 1540

commit v3 on v2

--- a/solution.py
+++ b/solution.py
@@ -47,11 +47,9 @@
     band_hbm, square_hbm, gain_hbm, wag_hbm, wa_hbm, wbg_hbm, wb_hbm, out_ref, band_norm,
     band, square, gain_ref, weights, normed, square_norm, held, sems,
 ):
-    quarter = band.shape[0] // 4
-    parts = [slice(n * quarter, n * quarter + quarter) for n in range(4)]
-    pairs = [(gain_hbm, gain_ref)]
-    pairs += [(band_hbm.at[part], band.at[part]) for part in parts]
-    pairs += [
+    pairs = [
+        (gain_hbm, gain_ref),
+        (band_hbm, band),
         (wag_hbm, weights.at[0]),
         (wa_hbm, weights.at[1]),
         (wbg_hbm, weights.at[2]),
@@ -74,14 +72,14 @@
         var = jnp.mean(centred * centred, axis=-1, keepdims=True)
         return centred * lax.rsqrt(var + 1e-05) * gain
 
-    for part in range(24):
-        if part % 6 == 0:
-            copies[1 + part // 6].wait()
-        rows = slice(part * LANES, part * LANES + LANES)
+    copies[1].wait()
+    half = band.shape[0] // 2
+    for part in range(2):
+        rows = slice(part * half, part * half + half)
         norm = normalise(band[rows, :])
         normed[rows, :] = norm
         band_norm[rows, :] = norm.astype(BF16)
-    for copy in copies[5:]:
+    for copy in copies[2:]:
         copy.wait()
     for step in range(9):
         k3, hi = step // 3, step % 3 * 2
@@ -262,7 +260,7 @@
             pltpu.VMEM((rows, LANES), F32),
             pltpu.VMEM((9, 2 * LANES, LANES), BF16),
             pltpu.VMEM((LANES * MESSAGE, LANES), F32),
-            pltpu.SemaphoreType.DMA((10,)),
+            pltpu.SemaphoreType.DMA((7,)),
         ],
         compiler_params=params(),
         name="edges",

time: 94.1 us -> 93.6 us (level)
  no operation moved by 1% of the time
where the time goes in v3:
time: 93.6 us; the launch traced here: 93.5 us
  blocking collectives  84.5 us (90%)
  Pallas kernels  7.93 us (8%)
    all_to_all x2, blocking collectives, exchange(): lax.all_to_all(values, CHIPS, split_axis=0, concat_axis=0, tiled=True)  84.5 us
    pallas_call x1, Pallas kernels, shards(): pl.pallas_call(edges_kernel, out_shape=(pltpu.VMEM((LANES * MESSAGE, LANE...  3.34 us
  transfers between devices with their start and end apart: 1, of which 1 were waited for; matrix products, arithmetic and copies ran while one was open for 0% of the time, Pallas kernels for 1%

profile of v3, /device:TPU:8, one launch (start us, length us, event | category | flops | bytes accessed | tf_op | source)
XLA Modules:
  0.0 93.5 jit_solution(12044386773964897000)
XLA Ops:
  0.0 3.3 %edges.1 = (bf16[5376,128]{1,0:T(8,128)(2,1)S(1)}, bf16[3072,128]{1,0:T(8,128)(2,1)S(1)}) custom-call(bf16[3072,128]{1,0:T(8,128)(2,1)} %bitcast.11, bf16[48,48,128]{2,1,0:T(8,128)(2,1)} %square_hbm.1, f32[1,128]{1,0:T(1,128)} %bitcast.12, bf16[128,128]{1,0:T(8,128)(2,1)} %wag_hbm.1, bf16[128,128]{1,0:T(8,128)(2,1)} %wa_hbm.1, bf16[128,128]{1,0:T(8,128)(2,1)} %wbg_hbm.1, ...), custom_call_target="tpu_custom_call" | custom-call | tf_op jit(solution)/shard_map/edges/pallas_call | solution.py:247
  3.3 52.8 %all_to_all.10 = bf16[128,21,2,128]{3,2,1,0:T(2,128)(2,1)S(1)} all-to-all(bf16[128,21,2,128]{3,2,1,0:T(2,128)(2,1)S(1)} %bitcast.9), channel_id=1, replica_groups=mesh['z'=8,'y_lo'=2,'x'=4,'y_hi'=2,'core'=2] {'z','y_lo','x','y_hi'}, dimensions={0} | all-to-all | bytes 2752512 | tf_op jit(solution)/shard_map/all_to_all | solution.py:237
  56.1 1.2 %product.1 = (bf16[384,1024]{1,0:T(8,128)(2,1)S(1)}, bf16[4,384,256]{2,1,0:T(8,128)(2,1)S(1)}) custom-call(s32[1]{0:T(128)} %bitcast.2.core_ref, bf16[5376,128]{1,0:T(8,128)(2,1)S(1)} %bitcast.7), custom_call_target="tpu_custom_call" | custom-call | tf_op jit(solution)/shard_map/product/pallas_call | solution.py:275
  57.3 0.0 copy-start
  57.4 0.1 collective-permute-start
  57.5 1.0 %own.1.own_ref = f32[384,1024]{1,0:T(8,128)S(1)} custom-call(s32[1]{0:T(128)} %bitcast.2.core_ref, bf16[5376,128]{1,0:T(8,128)(2,1)S(1)} %bitcast.8, bf16[4,384,256]{2,1,0:T(8,128)(2,1)S(1)} %get-tuple-element.24.left), custom_call_target="tpu_custom_call" | custom-call | tf_op jit(solution)/shard_map/own/pallas_call | solution.py:290
  58.4 0.0 copy-done
  58.4 0.4 gate.1.gate_ref
  58.8 0.0 copy-start.1
  58.8 0.0 copy-start.2
  58.8 0.9 collective-permute-done.other_ref
  59.7 0.3 sum.1
  60.1 31.7 %all_to_all.11.in_ref = bf16[128,24,128]{2,1,0:T(8,128)(2,1)S(1)} all-to-all(bf16[128,24,128]{2,1,0:T(8,128)(2,1)S(1)} %sum.1), channel_id=1, replica_groups=mesh['z'=8,'y_lo'=2,'x'=4,'y_hi'=2,'core'=2] {'z','y_lo','x','y_hi'}, dimensions={0} | all-to-all | bytes 1572864 | tf_op jit(solution)/shard_map/all_to_all | solution.py:237
  91.8 0.0 copy-done.1
  91.8 0.0 copy-done.2
  91.8 1.7 %update.1 = bf16[3072,128]{1,0:T(8,128)(2,1)} custom-call(bf16[128,24,128]{2,1,0:T(8,128)(2,1)S(1)} %all_to_all.11.in_ref, f32[3072,128]{1,0:T(8,128)S(1)} %gate.1.gate_ref, f32[1,128]{1,0:T(1,128)S(1)} %bitcast.10, bf16[128,128]{1,0:T(8,128)(2,1)S(1)} %copy-done.1), custom_call_target="tpu_custom_call" | custom-call | tf_op jit(solution)/shard_map/update/pallas_call | solution.py:317
Async XLA Ops:
  57.3 1.1 %copy-start = (bf16[128,128]{1,0:T(8,128)(2,1)S(1)}, bf16[128,128]{1,0:T(8,128)(2,1)}, u32[]{:S(2)}) copy-start(bf16[128,128]{1,0:T(8,128)(2,1)} %wg_ref.1) | copy-start | bytes 98308
  57.4 2.4 %collective-permute-start = (bf16[384,1024]{1,0:T(8,128)(2,1)S(1)}, bf16[384,1024]{1,0:T(8,128)(2,1)S(1)}, u32[]{:S(2)}, u32[]{:S(2)}) collective-permute-start(bf16[384,1024]{1,0:T(8,128)(2,1)S(1)} %get-tuple-element.25), channel_id=1, source_target_pairs={{0,1},{1,0},{2,3},{3,2},{4,5},{5,4},{6,7},{7,6},{8,9},{9,8},{10,11... | collective-permute-start | bytes 2359304 | tf_op jit(solution)/shard_map/ppermute | solution.py:289
  58.8 33.0 %copy-start.1 = (bf16[128,128]{1,0:T(8,128)(2,1)S(1)}, bf16[128,128]{1,0:T(8,128)(2,1)}, u32[]{:S(2)}) copy-start(bf16[128,128]{1,0:T(8,128)(2,1)} %wout_ref.1) | copy-start | bytes 98308
  58.8 33.0 %copy-start.2 = (f32[128]{0:T(128)S(1)}, f32[128]{0:T(128)}, u32[]{:S(2)}) copy-start(f32[128]{0:T(128)} %param.18) | copy-start | bytes 1540

commit v4 on v3

--- a/solution.py
+++ b/solution.py
@@ -10,7 +10,7 @@
 F32 = jnp.float32
 BF16 = jnp.bfloat16
 PARTS = (("z", 8), ("y_lo", 2), ("x", 4), ("y_hi", 2), ("core", 2))
-CHIPS = ("z", "y_lo", "x", "y_hi")
+AXES = tuple(name for name, _ in PARTS)
 ROWS = 16
 COLS = 8
 LANES = 128
@@ -234,7 +234,10 @@
 
 
 def exchange(values):
-    return lax.all_to_all(values, CHIPS, split_axis=0, concat_axis=0, tiled=True)
+    groups = [list(range(core, 2 * LANES, 2)) for core in range(2)]
+    return lax.all_to_all(
+        values, AXES, split_axis=0, concat_axis=0, axis_index_groups=groups, tiled=True
+    )
 
 
 def shards(z_band, z_square, ln_in_gain, w_a_gate, w_a, w_b_gate, w_b, w_g, ln_out_gain, w_out):
@@ -325,8 +328,7 @@
 
 
 def solution(mesh):
-    names = tuple(name for name, _ in PARTS)
-    fine = Mesh(mesh.devices.reshape(tuple(size for _, size in PARTS)), names)
+    fine = Mesh(mesh.devices.reshape(tuple(size for _, size in PARTS)), AXES)
     pair = P(("z", "y_lo"), ("x", "y_hi", "core"), None)
     placed = (pair, pair, P(), P(), P(), P(), P(), P(), P(), P())
     return jax.shard_map(

time: 93.6 us -> 93.6 us (level)
  no operation moved by 1% of the time
where the time goes in v4:
time: 93.6 us; the launch traced here: 93.5 us
  blocking collectives  84.5 us (90%)
  Pallas kernels  7.93 us (8%)
    all_to_all x2, blocking collectives, exchange(): lax.all_to_all(values, AXES, split_axis=0, concat_axis=0, axis_index_grou...  84.5 us
    pallas_call x1, Pallas kernels, shards(): pl.pallas_call(edges_kernel, out_shape=(pltpu.VMEM((LANES * MESSAGE, LANE...  3.34 us
  transfers between devices with their start and end apart: 1, of which 1 were waited for; matrix products, arithmetic and copies ran while one was open for 0% of the time, Pallas kernels for 1%

profile of v4, /device:TPU:8, one launch (start us, length us, event | category | flops | bytes accessed | tf_op | source)
XLA Modules:
  0.0 93.5 jit_solution(12044386773964897000)
XLA Ops:
  0.0 3.3 %edges.1 = (bf16[5376,128]{1,0:T(8,128)(2,1)S(1)}, bf16[3072,128]{1,0:T(8,128)(2,1)S(1)}) custom-call(bf16[3072,128]{1,0:T(8,128)(2,1)} %bitcast.11, bf16[48,48,128]{2,1,0:T(8,128)(2,1)} %square_hbm.1, f32[1,128]{1,0:T(1,128)} %bitcast.12, bf16[128,128]{1,0:T(8,128)(2,1)} %wag_hbm.1, bf16[128,128]{1,0:T(8,128)(2,1)} %wa_hbm.1, bf16[128,128]{1,0:T(8,128)(2,1)} %wbg_hbm.1, ...), custom_call_target="tpu_custom_call" | custom-call | tf_op jit(solution)/shard_map/edges/pallas_call | solution.py:250
  3.3 52.8 %all_to_all.10 = bf16[128,21,2,128]{3,2,1,0:T(2,128)(2,1)S(1)} all-to-all(bf16[128,21,2,128]{3,2,1,0:T(2,128)(2,1)S(1)} %bitcast.9), channel_id=1, replica_groups={{0,2,4,6,8,10,12,14,16,18,20,22,24,26,28,30,32,34,36,38,40,42,44,46,48,..., dimensions={0} | all-to-all | bytes 2752512 | tf_op jit(solution)/shard_map/all_to_all | solution.py:238
  56.1 1.2 %product.1 = (bf16[384,1024]{1,0:T(8,128)(2,1)S(1)}, bf16[4,384,256]{2,1,0:T(8,128)(2,1)S(1)}) custom-call(s32[1]{0:T(128)} %bitcast.2.core_ref, bf16[5376,128]{1,0:T(8,128)(2,1)S(1)} %bitcast.7), custom_call_target="tpu_custom_call" | custom-call | tf_op jit(solution)/shard_map/product/pallas_call | solution.py:278
  57.3 0.0 copy-start
  57.4 0.1 collective-permute-start
  57.5 1.0 %own.1.own_ref = f32[384,1024]{1,0:T(8,128)S(1)} custom-call(s32[1]{0:T(128)} %bitcast.2.core_ref, bf16[5376,128]{1,0:T(8,128)(2,1)S(1)} %bitcast.8, bf16[4,384,256]{2,1,0:T(8,128)(2,1)S(1)} %get-tuple-element.24.left), custom_call_target="tpu_custom_call" | custom-call | tf_op jit(solution)/shard_map/own/pallas_call | solution.py:293
  58.4 0.0 copy-done
  58.4 0.4 gate.1.gate_ref
  58.8 0.0 copy-start.1
  58.8 0.0 copy-start.2
  58.8 0.9 collective-permute-done.other_ref
  59.7 0.3 sum.1
  60.1 31.7 %all_to_all.11.in_ref = bf16[128,24,128]{2,1,0:T(8,128)(2,1)S(1)} all-to-all(bf16[128,24,128]{2,1,0:T(8,128)(2,1)S(1)} %sum.1), channel_id=1, replica_groups={{0,2,4,6,8,10,12,14,16,18,20,22,24,26,28,30,32,34,36,38,40,42,44,46,48,..., dimensions={0} | all-to-all | bytes 1572864 | tf_op jit(solution)/shard_map/all_to_all | solution.py:238
  91.8 0.0 copy-done.1
  91.8 0.0 copy-done.2
  91.8 1.7 %update.1 = bf16[3072,128]{1,0:T(8,128)(2,1)} custom-call(bf16[128,24,128]{2,1,0:T(8,128)(2,1)S(1)} %all_to_all.11.in_ref, f32[3072,128]{1,0:T(8,128)S(1)} %gate.1.gate_ref, f32[1,128]{1,0:T(1,128)S(1)} %bitcast.10, bf16[128,128]{1,0:T(8,128)(2,1)S(1)} %copy-done.1), custom_call_target="tpu_custom_call" | custom-call | tf_op jit(solution)/shard_map/update/pallas_call | solution.py:320
Async XLA Ops:
  57.3 1.1 %copy-start = (bf16[128,128]{1,0:T(8,128)(2,1)S(1)}, bf16[128,128]{1,0:T(8,128)(2,1)}, u32[]{:S(2)}) copy-start(bf16[128,128]{1,0:T(8,128)(2,1)} %wg_ref.1) | copy-start | bytes 98308
  57.4 2.4 %collective-permute-start = (bf16[384,1024]{1,0:T(8,128)(2,1)S(1)}, bf16[384,1024]{1,0:T(8,128)(2,1)S(1)}, u32[]{:S(2)}, u32[]{:S(2)}) collective-permute-start(bf16[384,1024]{1,0:T(8,128)(2,1)S(1)} %get-tuple-element.25), channel_id=1, source_target_pairs={{0,1},{1,0},{2,3},{3,2},{4,5},{5,4},{6,7},{7,6},{8,9},{9,8},{10,11... | collective-permute-start | bytes 2359304 | tf_op jit(solution)/shard_map/ppermute | solution.py:292
  58.8 33.0 %copy-start.1 = (bf16[128,128]{1,0:T(8,128)(2,1)S(1)}, bf16[128,128]{1,0:T(8,128)(2,1)}, u32[]{:S(2)}) copy-start(bf16[128,128]{1,0:T(8,128)(2,1)} %wout_ref.1) | copy-start | bytes 98308
  58.8 33.0 %copy-start.2 = (f32[128]{0:T(128)S(1)}, f32[128]{0:T(128)}, u32[]{:S(2)}) copy-start(f32[128]{0:T(128)} %param.18) | copy-start | bytes 1540

commit v5 on v3

--- a/solution.py
+++ b/solution.py
@@ -129,9 +129,8 @@
     for k3 in range(3):
         for hi in range(6):
             tiles = [held[half, pl.ds(k3 * 8 + hi, 8, stride=PITCH), :] for half in range(2)]
-            right[
-                hi * 64 + p * 16 : hi * 64 + p * 16 + 16, k3 * LANES : k3 * LANES + LANES
-            ] = jnp.concatenate(tiles, axis=0).astype(BF16)
+            start = (hi % 2 * 3 + hi // 2) * 64 + p * 16
+            right[start : start + 16, k3 * LANES : k3 * LANES + LANES] = jnp.concatenate(tiles, axis=0).astype(BF16)
 
 
 def multiply(right, left, out_ref):
@@ -209,24 +208,35 @@
     )
 
 
-def update_kernel(in_ref, gate_ref, gain_ref, wout_ref, out_ref, held, result):
+def update_kernel(in_ref, gate_ref, gain_ref, wout_ref, out_hbm, held, result, staged, sems):
     for h in range(LANES):
         held[h * PITCH : h * PITCH + 24, :] = in_ref[h].astype(F32)
     gain = jnp.broadcast_to(gain_ref[...], (LANES, LANES)).T
-    for j in range(24):
-        tri = held[pl.ds(j, LANES, stride=PITCH), :]
-        mean = jnp.mean(tri, axis=0, keepdims=True)
-        centred = tri - mean
-        var = jnp.mean(centred * centred, axis=0, keepdims=True)
-        normed = (centred * lax.rsqrt(var + 1e-05) * gain).astype(BF16)
-        projected = lax.dot_general(
-            normed, wout_ref[...], (((0,), (0,)), ((), ())), preferred_element_type=F32
+    copies = []
+    for jh in range(3):
+        for jl in range(8):
+            tri = held[pl.ds(jh * 8 + jl, LANES, stride=PITCH), :]
+            mean = jnp.mean(tri, axis=0, keepdims=True)
+            centred = tri - mean
+            var = jnp.mean(centred * centred, axis=0, keepdims=True)
+            normed = (centred * lax.rsqrt(var + 1e-05) * gain).astype(BF16)
+            projected = lax.dot_general(
+                normed, wout_ref[...], (((0,), (0,)), ((), ())), preferred_element_type=F32
+            )
+            for bit in range(2):
+                result[pl.ds(jh * 16 + bit * 8 + jl, 64, stride=49), :] = projected[
+                    bit * 64 : bit * 64 + 64
+                ]
+        block = slice(jh * 16, jh * 16 + 16)
+        for i in range(64):
+            start = i * 49 + jh * 16
+            staged[i, block, :] = (gate_ref[i, block, :] * result[start : start + 16, :]).astype(BF16)
+        copies.append(
+            pltpu.make_async_copy(staged.at[:, block, :], out_hbm.at[:, block, :], sems.at[jh])
         )
-        for bit in range(2):
-            result[pl.ds(bit * 24 + j, 64, stride=49), :] = projected[bit * 64 : bit * 64 + 64]
-    for i in range(64):
-        rows = slice(i * 48, i * 48 + 48)
-        out_ref[rows, :] = (gate_ref[rows, :] * result[i * 49 : i * 49 + 48, :]).astype(BF16)
+        copies[-1].start()
+    for copy in copies:
+        copy.wait()
 
 
 def shape(dims, kind):
@@ -314,14 +324,19 @@
     )(own, other)
     triangle, gate, gain_out = lax.optimization_barrier((triangle, gate, gain_out))
     triangle = exchange(triangle)
-    update = pl.pallas_call(
+    return pl.pallas_call(
         update_kernel,
-        out_shape=shape((rows, LANES), BF16),
-        scratch_shapes=[pltpu.VMEM((LANES * PITCH, LANES), F32), pltpu.VMEM((64 * 49, LANES), F32)],
+        out_shape=shape(z_band.shape, BF16),
+        out_specs=hbm,
+        scratch_shapes=[
+            pltpu.VMEM((LANES * PITCH, LANES), F32),
+            pltpu.VMEM((64 * 49, LANES), F32),
+            pltpu.VMEM(z_band.shape, BF16),
+            pltpu.SemaphoreType.DMA((3,)),
+        ],
         compiler_params=params(),
         name="update",
-    )(triangle, gate, gain_out, w_out)
-    return update.reshape(z_band.shape)
+    )(triangle, gate.reshape(z_band.shape), gain_out, w_out)
 
 
 def solution(mesh):

time: 93.6 us -> 93.6 us (level)
  no operation moved by 1% of the time
where the time goes in v5:
time: 93.6 us; the launch traced here: 93.4 us
  blocking collectives  84.5 us (90%)
  Pallas kernels  7.79 us (8%)
    all_to_all x2, blocking collectives, exchange(): lax.all_to_all(values, CHIPS, split_axis=0, concat_axis=0, tiled=True)  84.5 us
    pallas_call x1, Pallas kernels, shards(): pl.pallas_call(edges_kernel, out_shape=(pltpu.VMEM((LANES * MESSAGE, LANE...  3.34 us
  transfers between devices with their start and end apart: 1, of which 1 were waited for; matrix products, arithmetic and copies ran while one was open for 0% of the time, Pallas kernels for 1%

profile of v5, /device:TPU:8, one launch (start us, length us, event | category | flops | bytes accessed | tf_op | source)
XLA Modules:
  0.0 93.4 jit_solution(7288940621723945070)
XLA Ops:
  0.0 3.3 %edges.1 = (bf16[5376,128]{1,0:T(8,128)(2,1)S(1)}, bf16[3072,128]{1,0:T(8,128)(2,1)S(1)}) custom-call(bf16[3072,128]{1,0:T(8,128)(2,1)} %bitcast.12, bf16[48,48,128]{2,1,0:T(8,128)(2,1)} %square_hbm.1, f32[1,128]{1,0:T(1,128)} %bitcast.13, bf16[128,128]{1,0:T(8,128)(2,1)} %wag_hbm.1, bf16[128,128]{1,0:T(8,128)(2,1)} %wa_hbm.1, bf16[128,128]{1,0:T(8,128)(2,1)} %wbg_hbm.1, ...), custom_call_target="tpu_custom_call" | custom-call | tf_op jit(solution)/shard_map/edges/pallas_call | solution.py:257
  3.3 52.8 %all_to_all.10 = bf16[128,21,2,128]{3,2,1,0:T(2,128)(2,1)S(1)} all-to-all(bf16[128,21,2,128]{3,2,1,0:T(2,128)(2,1)S(1)} %bitcast.10), channel_id=1, replica_groups=mesh['z'=8,'y_lo'=2,'x'=4,'y_hi'=2,'core'=2] {'z','y_lo','x','y_hi'}, dimensions={0} | all-to-all | bytes 2752512 | tf_op jit(solution)/shard_map/all_to_all | solution.py:247
  56.1 1.2 %product.1 = (bf16[384,1024]{1,0:T(8,128)(2,1)S(1)}, bf16[4,384,256]{2,1,0:T(8,128)(2,1)S(1)}) custom-call(s32[1]{0:T(128)} %bitcast.2.core_ref, bf16[5376,128]{1,0:T(8,128)(2,1)S(1)} %bitcast.7), custom_call_target="tpu_custom_call" | custom-call | tf_op jit(solution)/shard_map/product/pallas_call | solution.py:285
  57.3 0.0 copy-start
  57.4 0.1 collective-permute-start
  57.5 1.0 %own.1.own_ref = f32[384,1024]{1,0:T(8,128)S(1)} custom-call(s32[1]{0:T(128)} %bitcast.2.core_ref, bf16[5376,128]{1,0:T(8,128)(2,1)S(1)} %bitcast.8, bf16[4,384,256]{2,1,0:T(8,128)(2,1)S(1)} %get-tuple-element.24.left), custom_call_target="tpu_custom_call" | custom-call | tf_op jit(solution)/shard_map/own/pallas_call | solution.py:300
  58.4 0.0 copy-done
  58.4 0.4 gate.1
  58.8 0.9 collective-permute-done.other_ref
  59.7 0.3 sum.1
  60.1 0.0 copy-start.1
  60.1 0.0 copy-start.2
  60.1 31.7 %all_to_all.11.in_ref = bf16[128,24,128]{2,1,0:T(8,128)(2,1)S(1)} all-to-all(bf16[128,24,128]{2,1,0:T(8,128)(2,1)S(1)} %sum.1), channel_id=1, replica_groups=mesh['z'=8,'y_lo'=2,'x'=4,'y_hi'=2,'core'=2] {'z','y_lo','x','y_hi'}, dimensions={0} | all-to-all | bytes 1572864 | tf_op jit(solution)/shard_map/all_to_all | solution.py:247
  91.8 0.0 copy-done.1
  91.8 0.0 copy-done.2
  91.8 1.6 %update.1 = bf16[64,48,128]{2,1,0:T(8,128)(2,1)} custom-call(bf16[128,24,128]{2,1,0:T(8,128)(2,1)S(1)} %all_to_all.11.in_ref, f32[64,48,128]{2,1,0:T(8,128)S(1)} %bitcast.9, f32[1,128]{1,0:T(1,128)S(1)} %bitcast.11, bf16[128,128]{1,0:T(8,128)(2,1)S(1)} %copy-done.1), custom_call_target="tpu_custom_call" | custom-call | tf_op jit(solution)/shard_map/update/pallas_call | solution.py:327
Async XLA Ops:
  57.3 1.1 %copy-start = (bf16[128,128]{1,0:T(8,128)(2,1)S(1)}, bf16[128,128]{1,0:T(8,128)(2,1)}, u32[]{:S(2)}) copy-start(bf16[128,128]{1,0:T(8,128)(2,1)} %wg_ref.1) | copy-start | bytes 98308
  57.4 2.4 %collective-permute-start = (bf16[384,1024]{1,0:T(8,128)(2,1)S(1)}, bf16[384,1024]{1,0:T(8,128)(2,1)S(1)}, u32[]{:S(2)}, u32[]{:S(2)}) collective-permute-start(bf16[384,1024]{1,0:T(8,128)(2,1)S(1)} %get-tuple-element.25), channel_id=1, source_target_pairs={{0,1},{1,0},{2,3},{3,2},{4,5},{5,4},{6,7},{7,6},{8,9},{9,8},{10,11... | collective-permute-start | bytes 2359304 | tf_op jit(solution)/shard_map/ppermute | solution.py:299
  60.1 31.7 %copy-start.1 = (bf16[128,128]{1,0:T(8,128)(2,1)S(1)}, bf16[128,128]{1,0:T(8,128)(2,1)}, u32[]{:S(2)}) copy-start(bf16[128,128]{1,0:T(8,128)(2,1)} %wout_ref.1) | copy-start | bytes 98308
  60.1 31.7 %copy-start.2 = (f32[128]{0:T(128)S(1)}, f32[128]{0:T(128)}, u32[]{:S(2)}) copy-start(f32[128]{0:T(128)} %param.18) | copy-start | bytes 1540

commit v6 on v5

--- a/solution.py
+++ b/solution.py
@@ -133,14 +133,14 @@
             right[start : start + 16, k3 * LANES : k3 * LANES + LANES] = jnp.concatenate(tiles, axis=0).astype(BF16)
 
 
-def multiply(right, left, out_ref):
-    for p in range(4):
-        out_ref[:, p * 256 : p * 256 + 256] = jnp.dot(
+def multiply(right, left, out_ref, parts=range(4)):
+    for n, p in enumerate(parts):
+        out_ref[:, n * 256 : n * 256 + 256] = jnp.dot(
             right[...], left[p], preferred_element_type=F32
         ).astype(out_ref.dtype)
 
 
-def product_kernel(core_ref, in_ref, other_ref, left, right, raw, held):
+def product_kernel(core_ref, in_ref, first_ref, second_ref, left, right, raw, held):
     size = 32 * MESSAGE
     there = pl.multiple_of((1 - core_ref[0]) * (8 * MESSAGE), 8)
 
@@ -165,7 +165,8 @@
                         half * LANES : half * LANES + LANES,
                     ] = jnp.concatenate(blocks[2 * k3 : 2 * k3 + 2], axis=0).astype(BF16)
         arrange_right(right_rows, right, held.at[p], p)
-    multiply(right, left, other_ref)
+    multiply(right, left, first_ref, (0, 1))
+    multiply(right, left, second_ref, (2, 3))
 
 
 def own_kernel(core_ref, in_ref, left, own_ref, right, raw, held):
@@ -184,14 +185,16 @@
     multiply(right, left, own_ref)
 
 
-def sum_kernel(own_ref, other_ref, out_ref):
+def sum_kernel(own_ref, first_ref, second_ref, out_ref):
     for p in range(8):
+        other_ref = (first_ref, second_ref)[p // 4]
         lanes = slice(p * LANES, p * LANES + LANES)
+        there = slice(p % 4 * LANES, p % 4 * LANES + LANES)
         for q2 in range(4):
             tiles = []
             for jh in range(3):
                 a, b = [
-                    own_ref[start : start + 16, lanes] + other_ref[start : start + 16, lanes].astype(F32)
+                    own_ref[start : start + 16, lanes] + other_ref[start : start + 16, there].astype(F32)
                     for start in (jh * 64 + q2 * 16, 192 + jh * 64 + q2 * 16)
                 ]
                 tiles.append(swap_halves(a, b))
@@ -282,11 +285,15 @@
     edges, core = lax.optimization_barrier((edges, core))
     edges = exchange(edges.reshape(LANES, MESSAGE // 2, 2, LANES)).reshape(edges.shape)
     smem = pl.BlockSpec(memory_space=pltpu.SMEM)
-    other, left = pl.pallas_call(
+    first, second, left = pl.pallas_call(
         product_kernel,
-        out_shape=(pltpu.VMEM((384, 1024), BF16), pltpu.VMEM((4, 384, 256), BF16)),
+        out_shape=(
+            pltpu.VMEM((384, 512), BF16),
+            pltpu.VMEM((384, 512), BF16),
+            pltpu.VMEM((4, 384, 256), BF16),
+        ),
         in_specs=[smem, vmem],
-        out_specs=(vmem, vmem),
+        out_specs=(vmem, vmem, vmem),
         scratch_shapes=[
             pltpu.VMEM((384, 384), BF16),
             pltpu.VMEM((4, 32 * MESSAGE + 8, LANES), F32),
@@ -295,8 +302,11 @@
         compiler_params=params(),
         name="product",
     )(core, edges)
-    other, left, band_norm, gain_out = lax.optimization_barrier((other, left, band_norm, gain_out))
-    other = lax.ppermute(other, "core", ((0, 1), (1, 0)))
+    first, second, left, band_norm, gain_out = lax.optimization_barrier(
+        (first, second, left, band_norm, gain_out)
+    )
+    first = lax.ppermute(first, "core", ((0, 1), (1, 0)))
+    second = lax.ppermute(second, "core", ((0, 1), (1, 0)))
     own = pl.pallas_call(
         own_kernel,
         out_shape=pltpu.VMEM((384, 1024), F32),
@@ -321,7 +331,7 @@
         out_shape=pltpu.VMEM((LANES, 24, LANES), BF16),
         compiler_params=params(),
         name="sum",
-    )(own, other)
+    )(own, first, second)
     triangle, gate, gain_out = lax.optimization_barrier((triangle, gate, gain_out))
     triangle = exchange(triangle)
     return pl.pallas_call(

time: 93.6 us -> 93.6 us (level)
  transfers between devices with their start and end apart: 1 -> 2, of which waited for: 1 -> 1; matrix products, arithmetic and copies ran while one was open for 0% -> 0% of each run, Pallas kernels for 1% -> 1%
where the time goes in v6:
time: 93.6 us; the launch traced here: 93.4 us
  blocking collectives  84.5 us (90%)
  Pallas kernels  7.81 us (8%)
    all_to_all x2, blocking collectives, exchange(): lax.all_to_all(values, CHIPS, split_axis=0, concat_axis=0, tiled=True)  84.5 us
    pallas_call x1, Pallas kernels, shards(): pl.pallas_call(edges_kernel, out_shape=(pltpu.VMEM((LANES * MESSAGE, LANE...  3.34 us
  transfers between devices with their start and end apart: 2, of which 1 were waited for; matrix products, arithmetic and copies ran while one was open for 0% of the time, Pallas kernels for 1%

profile of v6, /device:TPU:8, one launch (start us, length us, event | category | flops | bytes accessed | tf_op | source)
XLA Modules:
  0.0 93.4 jit_solution(13813065107927058068)
XLA Ops:
  0.0 3.3 %edges.1 = (bf16[5376,128]{1,0:T(8,128)(2,1)S(1)}, bf16[3072,128]{1,0:T(8,128)(2,1)S(1)}) custom-call(bf16[3072,128]{1,0:T(8,128)(2,1)} %bitcast.12, bf16[48,48,128]{2,1,0:T(8,128)(2,1)} %square_hbm.1, f32[1,128]{1,0:T(1,128)} %bitcast.13, bf16[128,128]{1,0:T(8,128)(2,1)} %wag_hbm.1, bf16[128,128]{1,0:T(8,128)(2,1)} %wa_hbm.1, bf16[128,128]{1,0:T(8,128)(2,1)} %wbg_hbm.1, ...), custom_call_target="tpu_custom_call" | custom-call | tf_op jit(solution)/shard_map/edges/pallas_call | solution.py:260
  3.3 52.8 %all_to_all.10 = bf16[128,21,2,128]{3,2,1,0:T(2,128)(2,1)S(1)} all-to-all(bf16[128,21,2,128]{3,2,1,0:T(2,128)(2,1)S(1)} %bitcast.10), channel_id=1, replica_groups=mesh['z'=8,'y_lo'=2,'x'=4,'y_hi'=2,'core'=2] {'z','y_lo','x','y_hi'}, dimensions={0} | all-to-all | bytes 2752512 | tf_op jit(solution)/shard_map/all_to_all | solution.py:250
  56.1 1.2 %product.1 = (bf16[384,512]{1,0:T(8,128)(2,1)S(1)}, bf16[384,512]{1,0:T(8,128)(2,1)S(1)}, bf16[4,384,256]{2,1,0:T(8,128)(2,1)S(1)}) custom-call(s32[1]{0:T(128)} %bitcast.2.core_ref, bf16[5376,128]{1,0:T(8,128)(2,1)S(1)} %bitcast.7), custom_call_target="tpu_custom_call" | custom-call | tf_op jit(solution)/shard_map/product/pallas_call | solution.py:288
  57.3 0.0 copy-start
  57.4 0.1 collective-permute-start
  57.5 0.5 collective-permute-start.1
  57.9 1.0 %own.1.own_ref = f32[384,1024]{1,0:T(8,128)S(1)} custom-call(s32[1]{0:T(128)} %bitcast.2.core_ref, bf16[5376,128]{1,0:T(8,128)(2,1)S(1)} %bitcast.8, bf16[4,384,256]{2,1,0:T(8,128)(2,1)S(1)} %get-tuple-element.27.left), custom_call_target="tpu_custom_call" | custom-call | tf_op jit(solution)/shard_map/own/pallas_call | solution.py:310
  58.9 0.0 copy-done
  58.9 0.4 gate.1
  59.3 0.0 collective-permute-done.first_ref
  59.3 0.4 collective-permute-done.1.second_ref
  59.7 0.4 sum.1
  60.1 0.0 copy-start.1
  60.1 0.0 copy-start.2
  60.1 31.7 %all_to_all.11.in_ref = bf16[128,24,128]{2,1,0:T(8,128)(2,1)S(1)} all-to-all(bf16[128,24,128]{2,1,0:T(8,128)(2,1)S(1)} %sum.1), channel_id=1, replica_groups=mesh['z'=8,'y_lo'=2,'x'=4,'y_hi'=2,'core'=2] {'z','y_lo','x','y_hi'}, dimensions={0} | all-to-all | bytes 1572864 | tf_op jit(solution)/shard_map/all_to_all | solution.py:250
  91.8 0.0 copy-done.1
  91.8 0.0 copy-done.2
  91.8 1.6 %update.1 = bf16[64,48,128]{2,1,0:T(8,128)(2,1)} custom-call(bf16[128,24,128]{2,1,0:T(8,128)(2,1)S(1)} %all_to_all.11.in_ref, f32[64,48,128]{2,1,0:T(8,128)S(1)} %bitcast.9, f32[1,128]{1,0:T(1,128)S(1)} %bitcast.11, bf16[128,128]{1,0:T(8,128)(2,1)S(1)} %copy-done.1), custom_call_target="tpu_custom_call" | custom-call | tf_op jit(solution)/shard_map/update/pallas_call | solution.py:337
Async XLA Ops:
  57.3 1.6 %copy-start = (bf16[128,128]{1,0:T(8,128)(2,1)S(1)}, bf16[128,128]{1,0:T(8,128)(2,1)}, u32[]{:S(2)}) copy-start(bf16[128,128]{1,0:T(8,128)(2,1)} %wg_ref.1) | copy-start | bytes 98308
  57.4 2.0 %collective-permute-start = (bf16[384,512]{1,0:T(8,128)(2,1)S(1)}, bf16[384,512]{1,0:T(8,128)(2,1)S(1)}, u32[]{:S(2)}, u32[]{:S(2)}) collective-permute-start(bf16[384,512]{1,0:T(8,128)(2,1)S(1)} %get-tuple-element.28), channel_id=1, source_target_pairs={{0,1},{1,0},{2,3},{3,2},{4,5},{5,4},{6,7},{7,6},{8,9},{9,8},{10,11... | collective-permute-start | bytes 1179656 | tf_op jit(solution)/shard_map/ppermute | solution.py:308
  57.5 2.3 %collective-permute-start.1 = (bf16[384,512]{1,0:T(8,128)(2,1)S(1)}, bf16[384,512]{1,0:T(8,128)(2,1)S(1)}, u32[]{:S(2)}, u32[]{:S(2)}) collective-permute-start(bf16[384,512]{1,0:T(8,128)(2,1)S(1)} %get-tuple-element.29), channel_id=1, source_target_pairs={{0,1},{1,0},{2,3},{3,2},{4,5},{5,4},{6,7},{7,6},{8,9},{9,8},{10,11... | collective-permute-start | bytes 1179656 | tf_op jit(solution)/shard_map/ppermute | solution.py:309
  60.1 31.7 %copy-start.1 = (bf16[128,128]{1,0:T(8,128)(2,1)S(1)}, bf16[128,128]{1,0:T(8,128)(2,1)}, u32[]{:S(2)}) copy-start(bf16[128,128]{1,0:T(8,128)(2,1)} %wout_ref.1) | copy-start | bytes 98308
  60.1 31.7 %copy-start.2 = (f32[128]{0:T(128)S(1)}, f32[128]{0:T(128)}, u32[]{:S(2)}) copy-start(f32[128]{0:T(128)} %param.18) | copy-start | bytes 1540

commit v7 on v5

--- a/solution.py
+++ b/solution.py
@@ -323,7 +323,7 @@
         name="sum",
     )(own, other)
     triangle, gate, gain_out = lax.optimization_barrier((triangle, gate, gain_out))
-    triangle = exchange(triangle)
+    triangle = exchange(triangle.reshape(LANES, 12, 2, LANES)).reshape(triangle.shape)
     return pl.pallas_call(
         update_kernel,
         out_shape=shape(z_band.shape, BF16),

time: 93.6 us -> 93.6 us (level)
  no operation moved by 1% of the time
where the time goes in v7:
time: 93.6 us; the launch traced here: 93.4 us
  blocking collectives  84.5 us (90%)
  Pallas kernels  7.79 us (8%)
    all_to_all x2, blocking collectives, exchange(): lax.all_to_all(values, CHIPS, split_axis=0, concat_axis=0, tiled=True)  84.5 us
    pallas_call x1, Pallas kernels, shards(): pl.pallas_call(edges_kernel, out_shape=(pltpu.VMEM((LANES * MESSAGE, LANE...  3.34 us
  transfers between devices with their start and end apart: 1, of which 1 were waited for; matrix products, arithmetic and copies ran while one was open for 0% of the time, Pallas kernels for 1%

profile of v7, /device:TPU:8, one launch (start us, length us, event | category | flops | bytes accessed | tf_op | source)
XLA Modules:
  0.0 93.4 jit_solution(7288940621723945070)
XLA Ops:
  0.0 3.3 %edges.1 = (bf16[5376,128]{1,0:T(8,128)(2,1)S(1)}, bf16[3072,128]{1,0:T(8,128)(2,1)S(1)}) custom-call(bf16[3072,128]{1,0:T(8,128)(2,1)} %bitcast.16, bf16[48,48,128]{2,1,0:T(8,128)(2,1)} %square_hbm.1, f32[1,128]{1,0:T(1,128)} %bitcast.17, bf16[128,128]{1,0:T(8,128)(2,1)} %wag_hbm.1, bf16[128,128]{1,0:T(8,128)(2,1)} %wa_hbm.1, bf16[128,128]{1,0:T(8,128)(2,1)} %wbg_hbm.1, ...), custom_call_target="tpu_custom_call" | custom-call | tf_op jit(solution)/shard_map/edges/pallas_call | solution.py:257
  3.3 52.8 %all_to_all.10 = bf16[128,21,2,128]{3,2,1,0:T(2,128)(2,1)S(1)} all-to-all(bf16[128,21,2,128]{3,2,1,0:T(2,128)(2,1)S(1)} %bitcast.14), channel_id=1, replica_groups=mesh['z'=8,'y_lo'=2,'x'=4,'y_hi'=2,'core'=2] {'z','y_lo','x','y_hi'}, dimensions={0} | all-to-all | bytes 2752512 | tf_op jit(solution)/shard_map/all_to_all | solution.py:247
  56.1 1.2 %product.1 = (bf16[384,1024]{1,0:T(8,128)(2,1)S(1)}, bf16[4,384,256]{2,1,0:T(8,128)(2,1)S(1)}) custom-call(s32[1]{0:T(128)} %bitcast.2.core_ref, bf16[5376,128]{1,0:T(8,128)(2,1)S(1)} %bitcast.9), custom_call_target="tpu_custom_call" | custom-call | tf_op jit(solution)/shard_map/product/pallas_call | solution.py:285
  57.3 0.0 copy-start
  57.4 0.1 collective-permute-start
  57.5 1.0 %own.1.own_ref = f32[384,1024]{1,0:T(8,128)S(1)} custom-call(s32[1]{0:T(128)} %bitcast.2.core_ref, bf16[5376,128]{1,0:T(8,128)(2,1)S(1)} %bitcast.10, bf16[4,384,256]{2,1,0:T(8,128)(2,1)S(1)} %get-tuple-element.24.left), custom_call_target="tpu_custom_call" | custom-call | tf_op jit(solution)/shard_map/own/pallas_call | solution.py:300
  58.4 0.0 copy-done
  58.4 0.4 gate.1
  58.8 0.9 collective-permute-done.other_ref
  59.7 0.3 sum.1
  60.1 0.0 copy-start.1
  60.1 0.0 copy-start.2
  60.1 31.7 %all_to_all.11 = bf16[128,12,2,128]{3,2,1,0:T(2,128)(2,1)S(1)} all-to-all(bf16[128,12,2,128]{3,2,1,0:T(2,128)(2,1)S(1)} %bitcast.12), channel_id=1, replica_groups=mesh['z'=8,'y_lo'=2,'x'=4,'y_hi'=2,'core'=2] {'z','y_lo','x','y_hi'}, dimensions={0} | all-to-all | bytes 1572864 | tf_op jit(solution)/shard_map/all_to_all | solution.py:247
  91.8 0.0 copy-done.1
  91.8 0.0 copy-done.2
  91.8 1.6 %update.1 = bf16[64,48,128]{2,1,0:T(8,128)(2,1)} custom-call(bf16[128,24,128]{2,1,0:T(8,128)(2,1)S(1)} %bitcast.13, f32[64,48,128]{2,1,0:T(8,128)S(1)} %bitcast.11, f32[1,128]{1,0:T(1,128)S(1)} %bitcast.15, bf16[128,128]{1,0:T(8,128)(2,1)S(1)} %copy-done.1), custom_call_target="tpu_custom_call" | custom-call | tf_op jit(solution)/shard_map/update/pallas_call | solution.py:327
Async XLA Ops:
  57.3 1.1 %copy-start = (bf16[128,128]{1,0:T(8,128)(2,1)S(1)}, bf16[128,128]{1,0:T(8,128)(2,1)}, u32[]{:S(2)}) copy-start(bf16[128,128]{1,0:T(8,128)(2,1)} %wg_ref.1) | copy-start | bytes 98308
  57.4 2.4 %collective-permute-start = (bf16[384,1024]{1,0:T(8,128)(2,1)S(1)}, bf16[384,1024]{1,0:T(8,128)(2,1)S(1)}, u32[]{:S(2)}, u32[]{:S(2)}) collective-permute-start(bf16[384,1024]{1,0:T(8,128)(2,1)S(1)} %get-tuple-element.25), channel_id=1, source_target_pairs={{0,1},{1,0},{2,3},{3,2},{4,5},{5,4},{6,7},{7,6},{8,9},{9,8},{10,11... | collective-permute-start | bytes 2359304 | tf_op jit(solution)/shard_map/ppermute | solution.py:299
  60.1 31.7 %copy-start.1 = (bf16[128,128]{1,0:T(8,128)(2,1)S(1)}, bf16[128,128]{1,0:T(8,128)(2,1)}, u32[]{:S(2)}) copy-start(bf16[128,128]{1,0:T(8,128)(2,1)} %wout_ref.1) | copy-start | bytes 98308
  60.1 31.7 %copy-start.2 = (f32[128]{0:T(128)S(1)}, f32[128]{0:T(128)}, u32[]{:S(2)}) copy-start(f32[128]{0:T(128)} %param.18) | copy-start | bytes 1540
